TPU v7x, 32 devices: a whole 2x2x4 slice. The times are simulated.
32 devices in a mesh: sect: 4 (over y, x), dp: 4 (over z), tp: 2 (over core).
Axes of the slice: x: 2, y: 2, z: 4, core: 2. Of those that a mesh axis runs over, the one named last changes fastest.
Arguments:
- queries: bfloat16 [4, 64, 48, 128], P('dp', 'sect', 'tp'), may hold values from -250 to 250
- key_cache: bfloat16 [4, 64, 8, 192, 128], P('dp', 'sect', 'tp'), may hold values from -6 to 6
- cached_values: bfloat16 [4, 64, 8, 192, 128], P('dp', 'sect', 'tp'), may hold values from -12 to 12
- incoming_keys: bfloat16 [4, 64, 8, 128], P('dp', 'sect', 'tp'), may hold values from -12 to 12
- incoming_values: bfloat16 [4, 64, 8, 128], P('dp', 'sect', 'tp'), may hold values from -12 to 12
- lengths: int32 [4, 64], P('dp', 'sect'), may hold values from 2 to 192, as said below
- residual: bfloat16 [256, 6144], P('dp', ('sect', 'tp')), may hold values from -8 to 8
- out_proj: bfloat16 [6144, 6144], P(None, ('sect', 'tp')), may hold values from -0.078125 to 0.078125
- norm_gain: float32 [6144], replicated, may hold values from 0.1 to 1.9
- router: bfloat16 [6144, 4], replicated, may hold values from -0.21875 to 0.21875
- gate_proj: bfloat16 [4, 6144, 8192], P('dp', 'sect', 'tp'), may hold values from -0.078125 to 0.078125
- up_proj: bfloat16 [4, 6144, 8192], P('dp', 'sect', 'tp'), may hold values from -0.078125 to 0.078125
- down_proj: bfloat16 [4, 8192, 6144], P('dp', 'tp', 'sect'), may hold values from -0.09375 to 0.09375
- routes: int32 [256, 2], P('dp'), may hold values from 0 to 3, as said below
Outputs:
- mixed: bfloat16 [256, 6144], P('dp', ('sect', 'tp'))
Inputs may be any that keep to these rules, and one draw needn't show every extreme that they name: `lengths`: each sequence has 2 or more filled slots; some sequence has all 192 filled. `routes`: the two experts of a token differ. In each block of 64 tokens held by one index of dp, no expert is named by more than 32 tokens, and the same expert is named by exactly 32 tokens in every block.
All inputs are finite; a program needn't handle non-finite values.
Results may differ from a plain program's by a relative error of at most 0.022.
Values may be sent and summed in bfloat16 or wider, within the bound.
A program may use at most 128 MiB of HBM per device.

v0:
```python
import math

import jax
import jax.numpy as jnp
from jax import lax
from jax.sharding import PartitionSpec as P

norm_epsilon = 1e-05


def attend(queries, key_cache, cached_values, incoming_keys, incoming_values, lengths):
    tokens = queries.shape[0]
    query_heads = queries.shape[1]
    head_size = queries.shape[2]
    kv_heads = key_cache.shape[1]
    heads_per_group = query_heads // kv_heads
    logit_scale = 1.0 / math.sqrt(head_size)
    query_head_groups = queries.reshape(tokens, kv_heads, heads_per_group, head_size)
    cached_entries = (
        jnp.einsum(
            "bkgd,bkpd->bkgp", query_head_groups, key_cache, preferred_element_type=jnp.float32
        )
        * logit_scale
    )
    new_token_score = (
        jnp.einsum(
            "ncwt,nct->ncw", query_head_groups, incoming_keys, preferred_element_type=jnp.float32
        )
        * logit_scale
    )
    positions = jnp.arange(key_cache.shape[2], dtype=jnp.int32)
    valid_slots = positions[None, :] < lengths[:, None]
    cached_entries = jnp.where(valid_slots[:, None, None, :], cached_entries, -jnp.inf)
    highest = jnp.maximum(jnp.max(cached_entries, axis=-1), new_token_score)
    cached_exp = jnp.exp(cached_entries - highest[..., None])
    fresh_exp = jnp.exp(new_token_score - highest)
    denominator = jnp.sum(cached_exp, axis=-1) + fresh_exp
    cached_prob = (cached_exp / denominator[..., None]).astype(jnp.bfloat16)
    fresh_prob = (fresh_exp / denominator).astype(jnp.bfloat16)
    gathered = jnp.einsum(
        "bkgp,bkpd->bkgd", cached_prob, cached_values, preferred_element_type=jnp.float32
    )
    gathered = (
        gathered
        + fresh_prob.astype(jnp.float32)[..., None]
        * incoming_values.astype(jnp.float32)[:, :, None, :]
    )
    return gathered.reshape(tokens, query_heads * head_size).astype(jnp.bfloat16)


def normalize(rows_in, norm_gain):
    values = rows_in.astype(jnp.float32)
    mean_square = jnp.mean(values * values, axis=-1, keepdims=True)
    return (values * lax.rsqrt(mean_square + norm_epsilon) * norm_gain).astype(jnp.bfloat16)


def width_share(rows_in):
    share = rows_in.shape[-1] // lax.axis_size("sect")
    return lax.dynamic_slice_in_dim(
        rows_in, lax.axis_index("sect") * share, share, rows_in.ndim - 1
    )


def expert_ffn(arrived, gate_proj, up_proj, down_proj):
    gate_pre = jnp.einsum("esnd,edf->esnf", arrived, gate_proj, preferred_element_type=jnp.float32)
    up_pre = jnp.einsum("esnd,edf->esnf", arrived, up_proj, preferred_element_type=jnp.float32)
    gate_total, up_total = lax.psum((gate_pre, up_pre), "sect")
    activated = (jax.nn.silu(gate_total) * up_total).astype(jnp.bfloat16)
    partial_out = jnp.einsum(
        "esnf,efd->esnd", activated, down_proj, preferred_element_type=jnp.float32
    )
    return lax.psum_scatter(partial_out.astype(jnp.bfloat16), "tp", scatter_dimension=3, tiled=True)


def per_device(
    queries,
    key_cache,
    cached_values,
    incoming_keys,
    incoming_values,
    lengths,
    residual,
    out_proj,
    norm_gain,
    router,
    gate_proj,
    up_proj,
    down_proj,
    routes,
):
    attended = attend(
        queries[0], key_cache[0], cached_values[0], incoming_keys[0], incoming_values[0], lengths[0]
    )
    seq_local = attended.shape[0]
    tp_count = lax.axis_size("tp")
    head_width = attended.shape[1]
    column_count = out_proj.shape[1]
    weight_split = out_proj.reshape(tp_count, head_width, column_count)
    initial = jnp.zeros((residual.shape[0], column_count), jnp.float32)
    shards = lax.all_gather(attended[None], ("sect", "tp"), axis=0, tiled=True)

    def add_one(counter, current):
        head_block = lax.dynamic_index_in_dim(shards, counter, 0, keepdims=False)
        weight = lax.dynamic_index_in_dim(weight_split, counter % tp_count, 0, keepdims=False)
        product = jnp.dot(head_block, weight, preferred_element_type=jnp.float32)
        row_start = counter // tp_count * seq_local
        earlier = lax.dynamic_slice_in_dim(current, row_start, seq_local, 0)
        return lax.dynamic_update_slice_in_dim(current, earlier + product, row_start, 0)

    projected = lax.fori_loop(0, shards.shape[0], add_one, initial)
    hidden = (residual.astype(jnp.float32) + projected).astype(jnp.bfloat16)
    group_rows = residual.shape[0]
    capacity = group_rows // 2
    expert_count = router.shape[1]
    slot_total = expert_count * capacity
    flat_routes = routes.reshape(-1)
    onehot = (flat_routes[:, None] == jnp.arange(expert_count, dtype=jnp.int32)[None, :]).astype(
        jnp.int32
    )
    earlier_count = jnp.cumsum(onehot, axis=0) - onehot
    target = flat_routes * capacity + jnp.sum(earlier_count * onehot, axis=1)
    matches = target[None, :] == jnp.arange(slot_total, dtype=jnp.int32)[:, None]
    route_token = jnp.arange(flat_routes.shape[0], dtype=jnp.int32) // 2
    slot_token = jnp.sum(jnp.where(matches, route_token[None, :], 0), axis=1)
    slot_used = jnp.any(matches, axis=1)
    full_width = lax.all_gather(hidden, ("sect", "tp"), axis=1, tiled=True)
    normed = normalize(full_width, norm_gain)
    logits = jnp.dot(normed, router, preferred_element_type=jnp.float32)
    chosen = jnp.take_along_axis(logits, routes, axis=1)
    mixing = jax.nn.sigmoid(chosen - chosen[:, ::-1])
    own_share = width_share(normed)
    taken = jnp.take(own_share, slot_token, axis=0)
    outgoing = jnp.where(slot_used[:, None], taken, jnp.zeros((), own_share.dtype)).reshape(
        expert_count, 1, capacity, own_share.shape[1]
    )
    returned = lax.all_to_all(
        expert_ffn(
            lax.all_to_all(outgoing, "dp", split_axis=0, concat_axis=1, tiled=True),
            gate_proj,
            up_proj,
            down_proj,
        ),
        "dp",
        split_axis=1,
        concat_axis=0,
        tiled=True,
    )
    mix_flat = mixing.reshape(-1)
    returned_rows = returned.reshape(slot_total, -1)[target].astype(jnp.float32)
    combined = jnp.sum(
        mix_flat.reshape(group_rows, 2)[:, :, None] * returned_rows.reshape(group_rows, 2, -1),
        axis=1,
    )
    return (hidden.astype(jnp.float32) + combined).astype(jnp.bfloat16)


def solution(mesh):
    placed = (
        P("dp", "sect", "tp", None),
        P("dp", "sect", "tp", None, None),
        P("dp", "sect", "tp", None, None),
        P("dp", "sect", "tp", None),
        P("dp", "sect", "tp", None),
        P("dp", "sect"),
        P("dp", ("sect", "tp")),
        P(None, ("sect", "tp")),
        P(),
        P(),
        P("dp", "sect", "tp"),
        P("dp", "sect", "tp"),
        P("dp", "tp", "sect"),
        P("dp", None),
    )
    return jax.shard_map(
        per_device, mesh=mesh, in_specs=placed, out_specs=P("dp", ("sect", "tp")), check_vma=False
    )
```

profile of v0, /device:TPU:0, one launch (start us, length us, event | category | flops | bytes accessed | tf_op | source)
XLA Modules:
  0.0 241.1 jit_solution(12203983700609856147)
XLA Ops:
  6.5 0.9 copy.66
  8.4 0.7 iota_compare_fusion.2
  9.1 0.7 bitcast_convert_fusion
  10.0 1.1 copy.61
  11.0 0.9 fusion.55
  11.9 1.8 fusion.66
  14.1 1.0 fusion.46
  15.3 11.9 %all_gather.6 = bf16[8,16,3072]{2,1,0:T(8,128)(2,1)S(1)} all-gather(bf16[1,16,3072]{2,1,0:T(8,128)(2,1)S(1)} %convert_element_type.76), channel_id=1, replica_groups=mesh['sect'=4,'dp'=4,'tp'=2] {'sect','tp'}, dimensions={0}, use_global_device_ids=true | all-gather | bytes 884736 | tf_op jit(solution)/shard_map/all_gather | solution.py:100
  27.2 24.5 %while.15 = (s32[]{:T(128)}, f32[64,768]{1,0:T(8,128)S(1)}, bf16[8,16,3072]{2,1,0:T(8,128)(2,1)S(1)}, bf16[2,3072,768]{2,1,0:T(8,128)(2,1)}, s32[]{:T(128)}, /*i...) while((s32[]{:T(128)}, f32[64,768]{1,0:T(8,128)S(1)}, bf16[8,16,3072]{2,1,0:T(8,128)(2,1)S(1)}, ...), condition=%wide.region_3.4_spmd, body=%wide.region_2.3_spmd.sunk | while | flops 75509776 | bytes 4915516 | solution.py:110
  27.2 3.1 %fusion.75 = f32[64,768]{1,0:T(8,128)S(1)} fusion(f32[64,768]{1,0:T(8,128)S(1)} %get-tuple-element.171, s32[]{:T(128)S(6)} %select_n.175, bf16[2,3072,768]{2,1,0:T(8,128)(2,1)} %get-tuple-element.183, s32[]{:T(128)S(6)} %select_n.177, bf16[8,16,3072]{2,1,0:T(8,128)(2,1)S(1)} %get-tuple-element.182, s32[]{:T(128)S(6)} %copy.83), kind=kOutput, calls=%fused_computation.7.clone.1 | convolution fusion | flops 75509760 | bytes 4915212 | tf_op jit(solution)/shard_map/while/body/eval_jaxpr/dot_general | solution.py:105
  30.3 3.1 %fusion.75 = f32[64,768]{1,0:T(8,128)S(1)} fusion(f32[64,768]{1,0:T(8,128)S(1)} %get-tuple-element.171, s32[]{:T(128)S(6)} %select_n.175, bf16[2,3072,768]{2,1,0:T(8,128)(2,1)} %get-tuple-element.183, s32[]{:T(128)S(6)} %select_n.177, bf16[8,16,3072]{2,1,0:T(8,128)(2,1)S(1)} %get-tuple-element.182, s32[]{:T(128)S(6)} %copy.83), kind=kOutput, calls=%fused_computation.7.clone.1 | convolution fusion | flops 75509760 | bytes 4915212 | tf_op jit(solution)/shard_map/while/body/eval_jaxpr/dot_general | solution.py:105
  33.3 3.1 %fusion.75 = f32[64,768]{1,0:T(8,128)S(1)} fusion(f32[64,768]{1,0:T(8,128)S(1)} %get-tuple-element.171, s32[]{:T(128)S(6)} %select_n.175, bf16[2,3072,768]{2,1,0:T(8,128)(2,1)} %get-tuple-element.183, s32[]{:T(128)S(6)} %select_n.177, bf16[8,16,3072]{2,1,0:T(8,128)(2,1)S(1)} %get-tuple-element.182, s32[]{:T(128)S(6)} %copy.83), kind=kOutput, calls=%fused_computation.7.clone.1 | convolution fusion | flops 75509760 | bytes 4915212 | tf_op jit(solution)/shard_map/while/body/eval_jaxpr/dot_general | solution.py:105
  36.4 3.1 %fusion.75 = f32[64,768]{1,0:T(8,128)S(1)} fusion(f32[64,768]{1,0:T(8,128)S(1)} %get-tuple-element.171, s32[]{:T(128)S(6)} %select_n.175, bf16[2,3072,768]{2,1,0:T(8,128)(2,1)} %get-tuple-element.183, s32[]{:T(128)S(6)} %select_n.177, bf16[8,16,3072]{2,1,0:T(8,128)(2,1)S(1)} %get-tuple-element.182, s32[]{:T(128)S(6)} %copy.83), kind=kOutput, calls=%fused_computation.7.clone.1 | convolution fusion | flops 75509760 | bytes 4915212 | tf_op jit(solution)/shard_map/while/body/eval_jaxpr/dot_general | solution.py:105
  39.5 3.1 %fusion.75 = f32[64,768]{1,0:T(8,128)S(1)} fusion(f32[64,768]{1,0:T(8,128)S(1)} %get-tuple-element.171, s32[]{:T(128)S(6)} %select_n.175, bf16[2,3072,768]{2,1,0:T(8,128)(2,1)} %get-tuple-element.183, s32[]{:T(128)S(6)} %select_n.177, bf16[8,16,3072]{2,1,0:T(8,128)(2,1)S(1)} %get-tuple-element.182, s32[]{:T(128)S(6)} %copy.83), kind=kOutput, calls=%fused_computation.7.clone.1 | convolution fusion | flops 75509760 | bytes 4915212 | tf_op jit(solution)/shard_map/while/body/eval_jaxpr/dot_general | solution.py:105
  42.5 3.1 %fusion.75 = f32[64,768]{1,0:T(8,128)S(1)} fusion(f32[64,768]{1,0:T(8,128)S(1)} %get-tuple-element.171, s32[]{:T(128)S(6)} %select_n.175, bf16[2,3072,768]{2,1,0:T(8,128)(2,1)} %get-tuple-element.183, s32[]{:T(128)S(6)} %select_n.177, bf16[8,16,3072]{2,1,0:T(8,128)(2,1)S(1)} %get-tuple-element.182, s32[]{:T(128)S(6)} %copy.83), kind=kOutput, calls=%fused_computation.7.clone.1 | convolution fusion | flops 75509760 | bytes 4915212 | tf_op jit(solution)/shard_map/while/body/eval_jaxpr/dot_general | solution.py:105
  45.6 3.1 %fusion.75 = f32[64,768]{1,0:T(8,128)S(1)} fusion(f32[64,768]{1,0:T(8,128)S(1)} %get-tuple-element.171, s32[]{:T(128)S(6)} %select_n.175, bf16[2,3072,768]{2,1,0:T(8,128)(2,1)} %get-tuple-element.183, s32[]{:T(128)S(6)} %select_n.177, bf16[8,16,3072]{2,1,0:T(8,128)(2,1)S(1)} %get-tuple-element.182, s32[]{:T(128)S(6)} %copy.83), kind=kOutput, calls=%fused_computation.7.clone.1 | convolution fusion | flops 75509760 | bytes 4915212 | tf_op jit(solution)/shard_map/while/body/eval_jaxpr/dot_general | solution.py:105
  48.6 3.1 %fusion.75 = f32[64,768]{1,0:T(8,128)S(1)} fusion(f32[64,768]{1,0:T(8,128)S(1)} %get-tuple-element.171, s32[]{:T(128)S(6)} %select_n.175, bf16[2,3072,768]{2,1,0:T(8,128)(2,1)} %get-tuple-element.183, s32[]{:T(128)S(6)} %select_n.177, bf16[8,16,3072]{2,1,0:T(8,128)(2,1)S(1)} %get-tuple-element.182, s32[]{:T(128)S(6)} %copy.83), kind=kOutput, calls=%fused_computation.7.clone.1 | convolution fusion | flops 75509760 | bytes 4915212 | tf_op jit(solution)/shard_map/while/body/eval_jaxpr/dot_general | solution.py:105
  51.7 11.3 %all_gather.7 = bf16[64,6144]{1,0:T(8,128)(2,1)S(1)} all-gather(bf16[64,768]{1,0:T(8,128)(2,1)S(1)} %add_convert_fusion.1), channel_id=1, replica_groups=mesh['sect'=4,'dp'=4,'tp'=2] {'sect','tp'}, dimensions={1}, use_global_device_ids=true | all-gather | bytes 884736 | tf_op jit(solution)/shard_map/all_gather | solution.py:126
  63.6 0.9 gather_fusion
  64.6 16.9 %all_to_all.8 = bf16[4,1,32,1536]{3,2,1,0:T(8,128)(2,1)S(1)} all-to-all(bf16[4,1,32,1536]{3,2,1,0:T(8,128)(2,1)S(1)} %select_select_fusion), channel_id=1, replica_groups=mesh['sect'=4,'dp'=4,'tp'=2] {'dp'}, dimensions={0} | all-to-all | bytes 786432 | tf_op jit(solution)/shard_map/all_to_all | solution.py:138
  81.5 7.7 %fusion.21 = f32[1,4,32,4096]{3,2,1,0:T(8,128)} fusion(bf16[1,1536,4096]{2,1,0:T(8,128)(2,1)} %param.27, bf16[4,1,32,1536]{3,2,1,0:T(8,128)(2,1)S(1)} %all_to_all.8), kind=kOutput, calls=%fused_computation.18 | convolution fusion | flops 1610612736 | bytes 15073280 | tf_op jit(solution)/shard_map/esnd,edf->esnf/dot_general | solution.py:66
  89.2 7.7 %fusion.18 = f32[1,4,32,4096]{3,2,1,0:T(8,128)} fusion(bf16[1,1536,4096]{2,1,0:T(8,128)(2,1)} %param.26, bf16[4,1,32,1536]{3,2,1,0:T(8,128)(2,1)S(1)} %all_to_all.8), kind=kOutput, calls=%fused_computation.17 | convolution fusion | flops 1610612736 | bytes 15073280 | tf_op jit(solution)/shard_map/esnd,edf->esnf/dot_general | solution.py:65
  97.6 101.8 %all-reduce.3.cloned.1.call-done = (f32[1,4,32,4096]{3,2,1,0:T(8,128)}, f32[1,4,32,4096]{3,2,1,0:T(8,128)}) async-done(((f32[1,4,32,4096]{3,2,1,0:T(8,128)}, f32[1,4,32,4096]{3,2,1,0:T(8,128)}), (f32[1,4,32,4096]{3,2,1,0:T(8,128)}, f32[1,4,32,4096]{3,2,1,0:T(8,128)})) %all-reduce.3.cloned.1.call-update) | async-done | bytes 4194320 | tf_op jit(solution)/shard_map/psum | solution.py:67
  199.4 8.6 %fusion.31 = bf16[1,4,32,1536]{3,2,1,0:T(8,128)(2,1)} fusion(bf16[1,4096,1536]{2,1,0:T(8,128)(2,1)} %param.28, f32[1,4,32,4096]{3,2,1,0:T(8,128)} %get-tuple-element.127, f32[1,4,32,4096]{3,2,1,0:T(8,128)} %get-tuple-element.128), kind=kOutput, calls=%fused_computation.24 | convolution fusion | flops 1613955072 | bytes 17170432 | tf_op jit(solution)/shard_map/esnf,efd->esnd/dot_general | solution.py:69
  208.9 1.5 gather_fusion.2
  211.4 4.6 %reduce-scatter.2.cloned.1.call-done = bf16[1,4,32,768]{3,2,1,0:T(8,128)(2,1)} async-done(((bf16[1,4,32,1536]{3,2,1,0:T(8,128)(2,1)}), bf16[1,4,32,768]{3,2,1,0:T(8,128)(2,1)}) %reduce-scatter.2.cloned.1.call-update) | async-done | bytes 196624 | tf_op jit(solution)/shard_map/reduce_scatter | solution.py:72
  216.0 4.9 %all-to-all-start.1 = ((bf16[1,4,32,768]{3,2,0,1:T(8,128)(2,1)}), bf16[1,4,32,768]{3,2,0,1:T(8,128)(2,1)S(1)}, u32[]{:S(2)}, u32[]{:S(2)}) async-start(bf16[1,4,32,768]{3,2,0,1:T(8,128)(2,1)} %bitcast.100), calls=%async_computation.2 | async-start | bytes 393216 | tf_op jit(solution)/shard_map/all_to_all | solution.py:136
  220.8 7.9 %all-to-all-done.1 = bf16[1,4,32,768]{3,2,0,1:T(8,128)(2,1)S(1)} async-done(((bf16[1,4,32,768]{3,2,0,1:T(8,128)(2,1)}), bf16[1,4,32,768]{3,2,0,1:T(8,128)(2,1)S(1)}, u32[]{:S(2)}, u32[]{:S(2)}) %all-to-all-start.1) | async-done | bytes 196640 | tf_op jit(solution)/shard_map/all_to_all | solution.py:136
  228.8 1.5 gather_fusion.1
  230.3 1.1 reshape.210
  231.4 1.3 multiply_reduce_fusion
  232.7 1.6 add_convert_fusion
  (58 shorter events, 4.6 us)
Async XLA Ops:
  6.5 5.4 %copy-start = (bf16[1,16,4,192,128]{4,3,2,1,0:T(8,128)(2,1)S(1)}, bf16[1,16,4,192,128]{4,3,2,1,0:T(8,128)(2,1)}, u32[]{:S(2)}) copy-start(bf16[1,16,4,192,128]{4,3,2,1,0:T(8,128)(2,1)} %param.17) | copy-start | bytes 9437188
  6.5 192.9 %all-reduce.3.cloned.1.call-start = ((), (), s32[]{:S(2)}) async-start(), calls=%async_computation.4 | async-start | bytes 8388608 | tf_op jit(solution)/shard_map/psum | solution.py:67
  9.9 4.2 %copy-start.6 = (bf16[1,16,4,192,128]{4,3,2,1,0:T(8,128)(2,1)S(1)}, bf16[1,16,4,192,128]{4,3,2,1,0:T(8,128)(2,1)}, u32[]{:S(2)}) copy-start(bf16[1,16,4,192,128]{4,3,2,1,0:T(8,128)(2,1)} %param.18) | copy-start | bytes 9437188
  27.1 24.6 %copy-start.3 = (bf16[64,768]{1,0:T(8,128)(2,1)S(1)}, bf16[64,768]{1,0:T(8,128)(2,1)}, u32[]{:S(2)}) copy-start(bf16[64,768]{1,0:T(8,128)(2,1)} %param.22) | copy-start | bytes 294916
  27.2 36.1 %copy-start.4 = (f32[6144]{0:T(1024)S(1)}, f32[6144]{0:T(1024)}, u32[]{:S(2)}) copy-start(f32[6144]{0:T(1024)} %param.24) | copy-start | bytes 73732
  51.7 11.5 %copy-start.2 = (bf16[64,768]{1,0:T(8,128)(2,1)}, bf16[64,768]{1,0:T(8,128)(2,1)S(1)}, u32[]{:S(2)}) copy-start(bf16[64,768]{1,0:T(8,128)(2,1)S(1)} %add_convert_fusion.1) | copy-start | bytes 294916
  96.9 0.7 copy-start.5
  96.9 119.0 %reduce-scatter.2.cloned.1.call-start = ((), (), s32[]{:S(2)}) async-start(), calls=%async_computation.3 | async-start | bytes 589824 | tf_op jit(solution)/shard_map/reduce_scatter | solution.py:72
  199.4 9.1 %copy-start.7 = (bf16[6144,4]{0,1:T(4,128)(2,1)S(1)}, bf16[6144,4]{0,1:T(4,128)(2,1)}, u32[]{:S(2)}) copy-start(bf16[6144,4]{0,1:T(4,128)(2,1)} %param.25) | copy-start | bytes 147460
  208.8 25.4 %copy-start.1 = (bf16[1,16,4,192,128]{4,3,2,1,0:T(8,128)(2,1)S(1)}, bf16[1,16,4,192,128]{4,3,2,1,0:T(8,128)(2,1)}, u32[]{:S(2)}) copy-start(bf16[1,16,4,192,128]{4,3,2,1,0:T(8,128)(2,1)} %param.17) | copy-start | bytes 9437188
  216.0 12.8 %all-to-all-start.1 = ((bf16[1,4,32,768]{3,2,0,1:T(8,128)(2,1)}), bf16[1,4,32,768]{3,2,0,1:T(8,128)(2,1)S(1)}, u32[]{:S(2)}, u32[]{:S(2)}) async-start(bf16[1,4,32,768]{3,2,0,1:T(8,128)(2,1)} %bitcast.100), calls=%async_computation.2 | async-start | bytes 393216 | tf_op jit(solution)/shard_map/all_to_all | solution.py:136
Sparse Core Ops, SparseCore 0:
  97.1 102.2 all-reduce.2
  208.2 7.7 reduce-scatter.1
where the time goes:
time: 242 us; the launch traced here: 241 us
  waiting for transfers between devices  114 us (47%)
  matrix products  52.6 us (22%)
  blocking collectives  40 us (17%)
  between operations  13.6 us (6%)
  local copies, waits for them, and re-layouts  9.4 us (4%)
  other arithmetic  6.04 us (2%)
  starting transfers between devices  5.08 us (2%)
    psum x1, waiting for transfers between devices, expert_ffn(): gate_total, up_total = lax.psum((gate_pre, up_pre), 'sect')  102 us
    dot_general x8, matrix products, add_one(): product = jnp.dot(head_block, weight, preferred_element_type=jnp.float32)  24.5 us
    all_to_all x1, blocking collectives, per_device(): lax.all_to_all(outgoing, 'dp', split_axis=0, concat_axis=1, tiled=True)  16.9 us
    all_gather x1, blocking collectives, per_device(): shards = lax.all_gather(attended[None], ('sect', 'tp'), axis=0, tiled=True)  11.9 us
    all_gather x1, blocking collectives, per_device(): full_width = lax.all_gather(hidden, ('sect', 'tp'), axis=1, tiled=True)  11.3 us
    dot_general x1, matrix products, expert_ffn(): jnp.einsum('esnf,efd->esnd', activated, down_proj, preferred_element_type...  8.61 us
    all_to_all x1, waiting for transfers between devices, per_device(): lax.all_to_all(expert_ffn(lax.all_to_all(outgoing, 'dp', split_axis=0, co...  7.93 us
    dot_general x1, matrix products, expert_ffn(): jnp.einsum('esnd,edf->esnf', arrived, gate_proj, preferred_element_type=j...  7.72 us
  transfers between devices with their start and end apart: 3, of which 3 were waited for; matrix products, arithmetic and copies ran while one was open for 1% of the time, Pallas kernels for 0%

commit v1 on v0

--- a/solution.py
+++ b/solution.py
@@ -64,8 +64,10 @@
 def expert_ffn(arrived, gate_proj, up_proj, down_proj):
     gate_pre = jnp.einsum("esnd,edf->esnf", arrived, gate_proj, preferred_element_type=jnp.float32)
     up_pre = jnp.einsum("esnd,edf->esnf", arrived, up_proj, preferred_element_type=jnp.float32)
-    gate_total, up_total = lax.psum((gate_pre, up_pre), "sect")
-    activated = (jax.nn.silu(gate_total) * up_total).astype(jnp.bfloat16)
+    pre = jnp.stack([gate_pre, up_pre]).astype(jnp.bfloat16)
+    total = lax.psum_scatter(pre, "sect", scatter_dimension=4, tiled=True).astype(jnp.float32)
+    share = (jax.nn.silu(total[0]) * total[1]).astype(jnp.bfloat16)
+    activated = lax.all_gather(share, "sect", axis=3, tiled=True)
     partial_out = jnp.einsum(
         "esnf,efd->esnd", activated, down_proj, preferred_element_type=jnp.float32
     )

time: 242 us -> 199 us (0.82)
  waiting for transfers between devices: 114 us -> 72.5 us
  matrix products: 52.6 us -> 48.7 us
  other arithmetic: 6.04 us -> 9.59 us
    psum x1 -> x0, waiting for transfers between devices: 102 us -> none  [expert_ffn(): gate_total, up_total = lax.psum((gate_pre, up_pre), 'sect')]
    reduce_scatter x0 -> x1, waiting for transfers between devices: none -> 33.4 us  [expert_ffn(): lax.psum_scatter(pre, 'sect', scatter_dimension=4, tiled=True)]
    all_gather x0 -> x1, waiting for transfers between devices: none -> 26.5 us  [expert_ffn(): activated = lax.all_gather(share, 'sect', axis=3, tiled=True)]
  transfers between devices with their start and end apart: 3 -> 4, of which waited for: 3 -> 4; matrix products, arithmetic and copies ran while one was open for 1% -> 2% of each run, Pallas kernels for 0% -> 0%
where the time goes in v1:
time: 199 us; the launch traced here: 198 us
  waiting for transfers between devices  72.5 us (36%)
  matrix products  48.7 us (24%)
  blocking collectives  40 us (20%)
  between operations  13.4 us (7%)
  other arithmetic  9.59 us (5%)
  local copies, waits for them, and re-layouts  8.99 us (5%)
  starting transfers between devices  5.12 us (3%)
    reduce_scatter x1, waiting for transfers between devices, expert_ffn(): lax.psum_scatter(pre, 'sect', scatter_dimension=4, tiled=True)  33.4 us
    all_gather x1, waiting for transfers between devices, expert_ffn(): activated = lax.all_gather(share, 'sect', axis=3, tiled=True)  26.5 us
    dot_general x8, matrix products, add_one(): product = jnp.dot(head_block, weight, preferred_element_type=jnp.float32)  24.5 us
    all_to_all x1, blocking collectives, per_device(): lax.all_to_all(outgoing, 'dp', split_axis=0, concat_axis=1, tiled=True)  16.9 us
    all_gather x1, blocking collectives, per_device(): shards = lax.all_gather(attended[None], ('sect', 'tp'), axis=0, tiled=True)  11.9 us
    all_gather x1, blocking collectives, per_device(): full_width = lax.all_gather(hidden, ('sect', 'tp'), axis=1, tiled=True)  11.3 us
    all_to_all x1, waiting for transfers between devices, per_device(): lax.all_to_all(expert_ffn(lax.all_to_all(outgoing, 'dp', split_axis=0, co...  7.93 us
    dot_general x1, matrix products, expert_ffn(): jnp.einsum('esnf,efd->esnd', activated, down_proj, preferred_element_type...  7.46 us
  transfers between devices with their start and end apart: 4, of which 4 were waited for; matrix products, arithmetic and copies ran while one was open for 2% of the time, Pallas kernels for 0%

profile of v1, /device:TPU:0, one launch (start us, length us, event | category | flops | bytes accessed | tf_op | source)
XLA Modules:
  0.0 198.4 jit_solution(2629832854828181565)
XLA Ops:
  6.5 0.9 copy.66
  10.0 1.1 copy.61
  11.0 0.9 fusion.63
  11.9 1.8 fusion.73
  14.1 1.0 fusion.52
  15.3 11.9 %all_gather.9 = bf16[8,16,3072]{2,1,0:T(8,128)(2,1)S(1)} all-gather(bf16[1,16,3072]{2,1,0:T(8,128)(2,1)S(1)} %convert_element_type.96), channel_id=1, replica_groups=mesh['sect'=4,'dp'=4,'tp'=2] {'sect','tp'}, dimensions={0}, use_global_device_ids=true | all-gather | bytes 884736 | tf_op jit(solution)/shard_map/all_gather | solution.py:102
  27.2 24.5 %while.15 = (s32[]{:T(128)}, f32[64,768]{1,0:T(8,128)S(1)}, bf16[8,16,3072]{2,1,0:T(8,128)(2,1)S(1)}, bf16[2,3072,768]{2,1,0:T(8,128)(2,1)}, s32[]{:T(128)}, /*i...) while((s32[]{:T(128)}, f32[64,768]{1,0:T(8,128)S(1)}, bf16[8,16,3072]{2,1,0:T(8,128)(2,1)S(1)}, ...), condition=%wide.region_3.4_spmd, body=%wide.region_2.3_spmd.sunk | while | flops 75509776 | bytes 4915516 | solution.py:112
  27.2 3.1 %fusion.82 = f32[64,768]{1,0:T(8,128)S(1)} fusion(f32[64,768]{1,0:T(8,128)S(1)} %get-tuple-element.169, s32[]{:T(128)S(6)} %select_n.175, bf16[2,3072,768]{2,1,0:T(8,128)(2,1)} %get-tuple-element.181, s32[]{:T(128)S(6)} %select_n.177, bf16[8,16,3072]{2,1,0:T(8,128)(2,1)S(1)} %get-tuple-element.180, s32[]{:T(128)S(6)} %copy.83), kind=kOutput, calls=%fused_computation.7.clone.1 | convolution fusion | flops 75509760 | bytes 4915212 | tf_op jit(solution)/shard_map/while/body/eval_jaxpr/dot_general | solution.py:107
  30.3 3.1 %fusion.82 = f32[64,768]{1,0:T(8,128)S(1)} fusion(f32[64,768]{1,0:T(8,128)S(1)} %get-tuple-element.169, s32[]{:T(128)S(6)} %select_n.175, bf16[2,3072,768]{2,1,0:T(8,128)(2,1)} %get-tuple-element.181, s32[]{:T(128)S(6)} %select_n.177, bf16[8,16,3072]{2,1,0:T(8,128)(2,1)S(1)} %get-tuple-element.180, s32[]{:T(128)S(6)} %copy.83), kind=kOutput, calls=%fused_computation.7.clone.1 | convolution fusion | flops 75509760 | bytes 4915212 | tf_op jit(solution)/shard_map/while/body/eval_jaxpr/dot_general | solution.py:107
  33.3 3.1 %fusion.82 = f32[64,768]{1,0:T(8,128)S(1)} fusion(f32[64,768]{1,0:T(8,128)S(1)} %get-tuple-element.169, s32[]{:T(128)S(6)} %select_n.175, bf16[2,3072,768]{2,1,0:T(8,128)(2,1)} %get-tuple-element.181, s32[]{:T(128)S(6)} %select_n.177, bf16[8,16,3072]{2,1,0:T(8,128)(2,1)S(1)} %get-tuple-element.180, s32[]{:T(128)S(6)} %copy.83), kind=kOutput, calls=%fused_computation.7.clone.1 | convolution fusion | flops 75509760 | bytes 4915212 | tf_op jit(solution)/shard_map/while/body/eval_jaxpr/dot_general | solution.py:107
  36.4 3.1 %fusion.82 = f32[64,768]{1,0:T(8,128)S(1)} fusion(f32[64,768]{1,0:T(8,128)S(1)} %get-tuple-element.169, s32[]{:T(128)S(6)} %select_n.175, bf16[2,3072,768]{2,1,0:T(8,128)(2,1)} %get-tuple-element.181, s32[]{:T(128)S(6)} %select_n.177, bf16[8,16,3072]{2,1,0:T(8,128)(2,1)S(1)} %get-tuple-element.180, s32[]{:T(128)S(6)} %copy.83), kind=kOutput, calls=%fused_computation.7.clone.1 | convolution fusion | flops 75509760 | bytes 4915212 | tf_op jit(solution)/shard_map/while/body/eval_jaxpr/dot_general | solution.py:107
  39.5 3.1 %fusion.82 = f32[64,768]{1,0:T(8,128)S(1)} fusion(f32[64,768]{1,0:T(8,128)S(1)} %get-tuple-element.169, s32[]{:T(128)S(6)} %select_n.175, bf16[2,3072,768]{2,1,0:T(8,128)(2,1)} %get-tuple-element.181, s32[]{:T(128)S(6)} %select_n.177, bf16[8,16,3072]{2,1,0:T(8,128)(2,1)S(1)} %get-tuple-element.180, s32[]{:T(128)S(6)} %copy.83), kind=kOutput, calls=%fused_computation.7.clone.1 | convolution fusion | flops 75509760 | bytes 4915212 | tf_op jit(solution)/shard_map/while/body/eval_jaxpr/dot_general | solution.py:107
  42.5 3.1 %fusion.82 = f32[64,768]{1,0:T(8,128)S(1)} fusion(f32[64,768]{1,0:T(8,128)S(1)} %get-tuple-element.169, s32[]{:T(128)S(6)} %select_n.175, bf16[2,3072,768]{2,1,0:T(8,128)(2,1)} %get-tuple-element.181, s32[]{:T(128)S(6)} %select_n.177, bf16[8,16,3072]{2,1,0:T(8,128)(2,1)S(1)} %get-tuple-element.180, s32[]{:T(128)S(6)} %copy.83), kind=kOutput, calls=%fused_computation.7.clone.1 | convolution fusion | flops 75509760 | bytes 4915212 | tf_op jit(solution)/shard_map/while/body/eval_jaxpr/dot_general | solution.py:107
  45.6 3.1 %fusion.82 = f32[64,768]{1,0:T(8,128)S(1)} fusion(f32[64,768]{1,0:T(8,128)S(1)} %get-tuple-element.169, s32[]{:T(128)S(6)} %select_n.175, bf16[2,3072,768]{2,1,0:T(8,128)(2,1)} %get-tuple-element.181, s32[]{:T(128)S(6)} %select_n.177, bf16[8,16,3072]{2,1,0:T(8,128)(2,1)S(1)} %get-tuple-element.180, s32[]{:T(128)S(6)} %copy.83), kind=kOutput, calls=%fused_computation.7.clone.1 | convolution fusion | flops 75509760 | bytes 4915212 | tf_op jit(solution)/shard_map/while/body/eval_jaxpr/dot_general | solution.py:107
  48.6 3.1 %fusion.82 = f32[64,768]{1,0:T(8,128)S(1)} fusion(f32[64,768]{1,0:T(8,128)S(1)} %get-tuple-element.169, s32[]{:T(128)S(6)} %select_n.175, bf16[2,3072,768]{2,1,0:T(8,128)(2,1)} %get-tuple-element.181, s32[]{:T(128)S(6)} %select_n.177, bf16[8,16,3072]{2,1,0:T(8,128)(2,1)S(1)} %get-tuple-element.180, s32[]{:T(128)S(6)} %copy.83), kind=kOutput, calls=%fused_computation.7.clone.1 | convolution fusion | flops 75509760 | bytes 4915212 | tf_op jit(solution)/shard_map/while/body/eval_jaxpr/dot_general | solution.py:107
  51.7 11.3 %all_gather.10 = bf16[64,6144]{1,0:T(8,128)(2,1)S(1)} all-gather(bf16[64,768]{1,0:T(8,128)(2,1)S(1)} %add_convert_fusion.1), channel_id=1, replica_groups=mesh['sect'=4,'dp'=4,'tp'=2] {'sect','tp'}, dimensions={1}, use_global_device_ids=true | all-gather | bytes 884736 | tf_op jit(solution)/shard_map/all_gather | solution.py:128
  64.6 16.9 %all_to_all.8 = bf16[4,1,32,1536]{3,2,1,0:T(8,128)(2,1)S(1)} all-to-all(bf16[4,1,32,1536]{3,2,1,0:T(8,128)(2,1)S(1)} %select_select_fusion), channel_id=1, replica_groups=mesh['sect'=4,'dp'=4,'tp'=2] {'dp'}, dimensions={0} | all-to-all | bytes 786432 | tf_op jit(solution)/shard_map/all_to_all | solution.py:140
  81.5 6.4 %fusion.24 = bf16[1,1,4,32,4096]{4,3,2,1,0:T(8,128)(2,1)S(1)} fusion(bf16[1,1536,4096]{2,1,0:T(8,128)(2,1)} %param.27, bf16[4,1,32,1536]{3,2,1,0:T(8,128)(2,1)S(1)} %all_to_all.8), kind=kOutput, calls=%fused_computation.19 | convolution fusion | flops 1611137024 | bytes 14024704 | tf_op jit(solution)/shard_map/esnd,edf->esnf/dot_general | solution.py:66
  87.9 6.4 %fusion.27 = bf16[1,1,4,32,4096]{4,3,2,1,0:T(8,128)(2,1)S(1)} fusion(bf16[1,1536,4096]{2,1,0:T(8,128)(2,1)} %param.26, bf16[4,1,32,1536]{3,2,1,0:T(8,128)(2,1)S(1)} %all_to_all.8), kind=kOutput, calls=%fused_computation.20 | convolution fusion | flops 1611137024 | bytes 14024704 | tf_op jit(solution)/shard_map/esnd,edf->esnf/dot_general | solution.py:65
  94.3 1.5 pad_maximum_fusion
  95.9 33.4 %reduce-scatter.3.cloned.1.call-done = bf16[2,1,4,32,1024]{4,3,2,1,0:T(8,128)(2,1)} async-done(((bf16[2,1,4,32,4096]{4,3,2,1,0:T(8,128)(2,1)}), bf16[2,1,4,32,1024]{4,3,2,1,0:T(8,128)(2,1)}) %reduce-scatter.3.cloned.1.call-update) | async-done | bytes 524304 | tf_op jit(solution)/shard_map/reduce_scatter | solution.py:68
  129.3 1.1 convert_element_type.102
  131.6 26.5 %all-gather.2.cloned.1.call-done = bf16[1,4,32,4096]{3,2,1,0:T(8,128)(2,1)} async-done(((bf16[1,4,32,1024]{3,2,1,0:T(8,128)(2,1)}), bf16[1,4,32,4096]{3,2,1,0:T(8,128)(2,1)}) %all-gather.2.cloned.1.call-update) | async-done | bytes 1048592 | tf_op jit(solution)/shard_map/all_gather | solution.py:70
  158.1 7.5 %fusion.37 = bf16[1,4,32,1536]{3,2,1,0:T(8,128)(2,1)} fusion(bf16[1,4096,1536]{2,1,0:T(8,128)(2,1)} %param.28, bf16[1,4,32,4096]{3,2,1,0:T(8,128)(2,1)} %all-gather.2.cloned.1.call-done), kind=kOutput, calls=%fused_computation.26 | convolution fusion | flops 1610809344 | bytes 14024704 | tf_op jit(solution)/shard_map/esnf,efd->esnd/dot_general | solution.py:71
  166.4 1.5 gather_fusion.2
  169.0 4.6 %reduce-scatter.5.cloned.1.call-done = bf16[1,4,32,768]{3,2,1,0:T(8,128)(2,1)} async-done(((bf16[1,4,32,1536]{3,2,1,0:T(8,128)(2,1)}), bf16[1,4,32,768]{3,2,1,0:T(8,128)(2,1)}) %reduce-scatter.5.cloned.1.call-update) | async-done | bytes 196624 | tf_op jit(solution)/shard_map/reduce_scatter | solution.py:74
  173.6 4.9 %all-to-all-start.1 = ((bf16[1,4,32,768]{3,2,0,1:T(8,128)(2,1)}), bf16[1,4,32,768]{3,2,0,1:T(8,128)(2,1)S(1)}, u32[]{:S(2)}, u32[]{:S(2)}) async-start(bf16[1,4,32,768]{3,2,0,1:T(8,128)(2,1)} %bitcast.114), calls=%async_computation.3 | async-start | bytes 393216 | tf_op jit(solution)/shard_map/all_to_all | solution.py:138
  178.4 7.9 %all-to-all-done.1 = bf16[1,4,32,768]{3,2,0,1:T(8,128)(2,1)S(1)} async-done(((bf16[1,4,32,768]{3,2,0,1:T(8,128)(2,1)}), bf16[1,4,32,768]{3,2,0,1:T(8,128)(2,1)S(1)}, u32[]{:S(2)}, u32[]{:S(2)}) %all-to-all-start.1) | async-done | bytes 196640 | tf_op jit(solution)/shard_map/all_to_all | solution.py:138
  186.4 1.5 gather_fusion.1
  187.9 1.1 reshape.302
  189.0 1.3 multiply_reduce_fusion
  190.3 1.6 add_convert_fusion
  (68 shorter events, 7.5 us)
Async XLA Ops:
  6.5 5.4 %copy-start = (bf16[1,16,4,192,128]{4,3,2,1,0:T(8,128)(2,1)S(1)}, bf16[1,16,4,192,128]{4,3,2,1,0:T(8,128)(2,1)}, u32[]{:S(2)}) copy-start(bf16[1,16,4,192,128]{4,3,2,1,0:T(8,128)(2,1)} %param.17) | copy-start | bytes 9437188
  6.5 122.8 %reduce-scatter.3.cloned.1.call-start = ((), (), s32[]{:S(2)}) async-start(), calls=%async_computation.4 | async-start | bytes 2621440 | tf_op jit(solution)/shard_map/reduce_scatter | solution.py:68
  9.9 4.2 %copy-start.8 = (bf16[1,16,4,192,128]{4,3,2,1,0:T(8,128)(2,1)S(1)}, bf16[1,16,4,192,128]{4,3,2,1,0:T(8,128)(2,1)}, u32[]{:S(2)}) copy-start(bf16[1,16,4,192,128]{4,3,2,1,0:T(8,128)(2,1)} %param.18) | copy-start | bytes 9437188
  27.1 24.6 %copy-start.5 = (bf16[64,768]{1,0:T(8,128)(2,1)S(1)}, bf16[64,768]{1,0:T(8,128)(2,1)}, u32[]{:S(2)}) copy-start(bf16[64,768]{1,0:T(8,128)(2,1)} %param.22) | copy-start | bytes 294916
  27.2 36.1 %copy-start.6 = (f32[6144]{0:T(1024)S(1)}, f32[6144]{0:T(1024)}, u32[]{:S(2)}) copy-start(f32[6144]{0:T(1024)} %param.24) | copy-start | bytes 73732
  51.7 11.5 %copy-start.4 = (bf16[64,768]{1,0:T(8,128)(2,1)}, bf16[64,768]{1,0:T(8,128)(2,1)S(1)}, u32[]{:S(2)}) copy-start(bf16[64,768]{1,0:T(8,128)(2,1)S(1)} %add_convert_fusion.1) | copy-start | bytes 294916
  63.5 1.1 copy-start.2
  95.8 35.8 %copy-start.7 = (s32[64,2]{0,1:T(2,128)S(1)}, s32[64,2]{0,1:T(2,128)}, u32[]{:S(2)}) copy-start(s32[64,2]{0,1:T(2,128)} %param.29) | copy-start | bytes 1540
  95.8 62.3 %all-gather.2.cloned.1.call-start = ((), (), s32[]{:S(2)}) async-start(), calls=%async_computation.5 | async-start | bytes 1310720 | tf_op jit(solution)/shard_map/all_gather | solution.py:70
  131.4 42.2 %reduce-scatter.5.cloned.1.call-start = ((), (), s32[]{:S(2)}) async-start(), calls=%async_computation.6 | async-start | bytes 589824 | tf_op jit(solution)/shard_map/reduce_scatter | solution.py:74
  131.6 34.5 %copy-start.3 = (bf16[64,6144]{1,0:T(8,128)(2,1)S(1)}, bf16[64,6144]{1,0:T(8,128)(2,1)}, u32[]{:S(2)}) copy-start(bf16[64,6144]{1,0:T(8,128)(2,1)} %copy-done.2) | copy-start | bytes 2359300
  131.6 34.5 %copy-start.9 = (bf16[6144,4]{0,1:T(4,128)(2,1)S(1)}, bf16[6144,4]{0,1:T(4,128)(2,1)}, u32[]{:S(2)}) copy-start(bf16[6144,4]{0,1:T(4,128)(2,1)} %param.25) | copy-start | bytes 147460
  166.4 25.4 %copy-start.1 = (bf16[1,16,4,192,128]{4,3,2,1,0:T(8,128)(2,1)S(1)}, bf16[1,16,4,192,128]{4,3,2,1,0:T(8,128)(2,1)}, u32[]{:S(2)}) copy-start(bf16[1,16,4,192,128]{4,3,2,1,0:T(8,128)(2,1)} %param.17) | copy-start | bytes 9437188
  173.6 12.8 %all-to-all-start.1 = ((bf16[1,4,32,768]{3,2,0,1:T(8,128)(2,1)}), bf16[1,4,32,768]{3,2,0,1:T(8,128)(2,1)S(1)}, u32[]{:S(2)}, u32[]{:S(2)}) async-start(bf16[1,4,32,768]{3,2,0,1:T(8,128)(2,1)} %bitcast.114), calls=%async_computation.3 | async-start | bytes 393216 | tf_op jit(solution)/shard_map/all_to_all | solution.py:138
Sparse Core Ops, SparseCore 0:
  96.0 33.3 reduce-scatter.2
  131.5 26.6 all-gather.1
  165.8 7.7 reduce-scatter.4

commit v2 on v1

--- a/solution.py
+++ b/solution.py
@@ -1,11 +1,16 @@
+import functools
 import math
 
 import jax
 import jax.numpy as jnp
 from jax import lax
+from jax.experimental import pallas as pl
+from jax.experimental.pallas import tpu as pltpu
 from jax.sharding import PartitionSpec as P
 
 norm_epsilon = 1e-05
+MESH = pl.DeviceIdType.MESH
+TILE = 256
 
 
 def attend(queries, key_cache, cached_values, incoming_keys, incoming_values, lengths):
@@ -72,6 +77,438 @@
         "esnf,efd->esnd", activated, down_proj, preferred_element_type=jnp.float32
     )
     return lax.psum_scatter(partial_out.astype(jnp.bfloat16), "tp", scatter_dimension=3, tiled=True)
+
+
+def layer_kernel(
+    sizes,
+    attended_ref,
+    residual_ref,
+    gain_ref,
+    router_ref,
+    routes_ref,
+    out_proj_hbm,
+    gate_hbm,
+    up_hbm,
+    down_hbm,
+    out_ref,
+    out_w,
+    gate_w,
+    up_w,
+    down_w,
+    att_all,
+    hidden,
+    hit,
+    outgoing,
+    arrived,
+    expert_in,
+    square_out,
+    square_in,
+    pre_out,
+    pre_in,
+    pre_own,
+    act_all,
+    down_own,
+    pair_out,
+    pair_in,
+    expert_out,
+    returned,
+    stat_out,
+    stat_in,
+    weight_sem,
+    att_send,
+    att_recv,
+    row_send,
+    row_recv,
+    stat_send,
+    stat_recv,
+    square_send,
+    square_recv,
+    pre_send,
+    pre_recv,
+    act_send,
+    act_recv,
+    pair_send,
+    pair_recv,
+    back_send,
+    back_recv,
+):
+    n_sect, n_dp, n_tp = sizes
+    sect = lax.axis_index("sect")
+    dp = lax.axis_index("dp")
+    tp = lax.axis_index("tp")
+    group = n_sect * n_tp
+    me = sect * n_tp + tp
+    f32, bf16 = jnp.float32, jnp.bfloat16
+
+    def flip(value, bits):
+        result = value
+        bit = 1
+        while bit <= bits:
+            if bits & bit:
+                result = result + bit - 2 * bit * ((value // bit) % 2)
+            bit *= 2
+        return result
+
+    def in_group(j):
+        other = flip(me, j)
+        return {"sect": other // n_tp, "dp": dp, "tp": other % n_tp}
+
+    def in_line(i, t):
+        return {"sect": sect, "dp": flip(dp, i), "tp": flip(tp, t)}
+
+    loads = []
+    for index, (source, target) in enumerate(
+        ((out_proj_hbm, out_w), (gate_hbm, gate_w), (up_hbm, up_w), (down_hbm, down_w))
+    ):
+        rows = source.shape[0] // 4
+        for part in range(4):
+            pltpu.make_async_copy(
+                source.at[pl.ds(part * rows, rows)],
+                target.at[pl.ds(part * rows, rows)],
+                weight_sem.at[index],
+            ).start()
+        loads.append(pltpu.make_async_copy(source, target, weight_sem.at[index]))
+
+    barrier = pltpu.get_barrier_semaphore()
+    for j in range(1, group):
+        pl.semaphore_signal(barrier, inc=1, device_id=in_group(j), device_id_type=MESH)
+    for i in range(1, n_dp):
+        for t in range(n_tp):
+            pl.semaphore_signal(barrier, inc=1, device_id=in_line(i, t), device_id_type=MESH)
+    pl.semaphore_wait(barrier, group - 1 + (n_dp - 1) * n_tp)
+
+    seq = attended_ref.shape[0]
+    own_rows = pl.ds(pl.multiple_of(sect * seq, seq), seq)
+    att_copies = []
+    for j in range(1, group):
+        copy = pltpu.make_async_remote_copy(
+            src_ref=attended_ref,
+            dst_ref=att_all.at[tp, own_rows],
+            send_sem=att_send.at[j],
+            recv_sem=att_recv.at[j],
+            device_id=in_group(j),
+            device_id_type=MESH,
+        )
+        copy.start()
+        att_copies.append(copy)
+    att_all[tp, own_rows, :] = attended_ref[...]
+
+    experts = router_ref.shape[0]
+    tokens = routes_ref.shape[1]
+    cap = tokens // 2
+    slots = experts * cap
+    choice = [routes_ref[k : k + 1, :] for k in range(2)]
+    expert_ids = lax.broadcasted_iota(jnp.int32, (8, tokens), 0)
+    onehot = [jnp.where(expert_ids == choice[k], 1.0, 0.0).astype(f32) for k in range(2)]
+    before = jnp.where(
+        lax.broadcasted_iota(jnp.int32, (tokens, tokens), 0)
+        < lax.broadcasted_iota(jnp.int32, (tokens, tokens), 1),
+        1.0,
+        0.0,
+    ).astype(bf16)
+    rank = jnp.dot((onehot[0] + onehot[1]).astype(bf16), before, preferred_element_type=f32)
+    slot_ids = lax.broadcasted_iota(jnp.int32, (slots, tokens), 0)
+    for k in range(2):
+        slot = jnp.sum(rank * onehot[k], axis=0, keepdims=True).astype(jnp.int32)
+        hit[k] = jnp.where(slot_ids == choice[k] * cap + slot, 1.0, 0.0).astype(f32)
+
+    loads[0].wait()
+    for copy in att_copies:
+        copy.wait_recv()
+
+    half = att_all.shape[2]
+    width = out_w.shape[1]
+
+    def project(n, carry):
+        columns = pl.ds(pl.multiple_of(n * TILE, TILE), TILE)
+        total = residual_ref[:, columns].astype(f32)
+        for t in range(n_tp):
+            total = total + jnp.dot(
+                att_all[t], out_w[t * half : (t + 1) * half, columns], preferred_element_type=f32
+            )
+        hidden[:, columns] = total.astype(bf16)
+        return carry
+
+    lax.fori_loop(0, width // TILE, project, 0)
+
+    rows = jnp.dot((hit[0] + hit[1]).astype(bf16), hidden[...], preferred_element_type=f32)
+    outgoing[...] = rows.astype(bf16).reshape(experts, cap, width)
+    line_rows = pl.ds(pl.multiple_of(dp * cap, cap), cap)
+    row_copies = []
+    for i in range(n_dp - 1, -1, -1):
+        for t in range(n_tp):
+            if i == 0 and t == 0:
+                continue
+            copy = pltpu.make_async_remote_copy(
+                src_ref=outgoing.at[flip(dp, i)],
+                dst_ref=arrived.at[tp, line_rows],
+                send_sem=row_send.at[i * n_tp + t],
+                recv_sem=row_recv.at[i * n_tp + t],
+                device_id=in_line(i, t),
+                device_id_type=MESH,
+            )
+            copy.start()
+            row_copies.append(copy)
+    arrived[tp, line_rows, :] = outgoing[dp]
+
+    own = hidden[...].astype(f32)
+    scaled = (own * gain_ref[me]).astype(bf16)
+    nt = (((1,), (1,)), ((), ()))
+    router_part = router_ref[:, pl.ds(pl.multiple_of(me * width, width), width)]
+    logit_part = lax.dot_general(router_part, scaled, nt, preferred_element_type=f32)
+    square = own * own
+    square_high = square.astype(bf16)
+    square_low = (square - square_high.astype(f32)).astype(bf16)
+    ones = jnp.ones((8, width), bf16)
+    square_part = lax.dot_general(
+        ones, square_high, nt, preferred_element_type=f32
+    ) + lax.dot_general(ones, square_low, nt, preferred_element_type=f32)
+    stat_out[...] = jnp.zeros_like(stat_out)
+    stat_out[0, 0:experts, 0:tokens] = logit_part
+    stat_out[1, :, 0:tokens] = square_part
+    stat_copies = []
+    for j in range(1, group):
+        copy = pltpu.make_async_remote_copy(
+            src_ref=stat_out,
+            dst_ref=stat_in.at[me],
+            send_sem=stat_send.at[j],
+            recv_sem=stat_recv.at[j],
+            device_id=in_group(j),
+            device_id_type=MESH,
+        )
+        copy.start()
+        stat_copies.append(copy)
+    stat_in[me] = stat_out[...]
+
+    for copy in row_copies:
+        copy.wait_recv()
+
+    total_square = jnp.zeros((arrived.shape[1], 1), f32)
+    for t in range(n_tp):
+        part = arrived[t].astype(f32)
+        total_square = total_square + jnp.sum(part * part, axis=1, keepdims=True)
+        expert_in[:, t * width : (t + 1) * width] = (part * gain_ref[sect * n_tp + t]).astype(bf16)
+    square_out[...] = jnp.broadcast_to(total_square, square_out.shape)
+    square_copies = []
+    for j in range(1, n_sect):
+        copy = pltpu.make_async_remote_copy(
+            src_ref=square_out,
+            dst_ref=square_in.at[j],
+            send_sem=square_send.at[j],
+            recv_sem=square_recv.at[j],
+            device_id={"sect": flip(sect, j), "dp": dp, "tp": tp},
+            device_id_type=MESH,
+        )
+        copy.start()
+        square_copies.append(copy)
+
+    loads[1].wait()
+    loads[2].wait()
+    share = act_all.shape[2]
+    pre_copies = []
+    for j in range(n_sect - 1, -1, -1):
+        partner = flip(sect, j)
+
+        def columns_of(n, carry):
+            source = pl.ds(pl.multiple_of(partner * share + n * TILE, TILE), TILE)
+            target = pl.ds(pl.multiple_of(n * TILE, TILE), TILE)
+            for which, weight in enumerate((gate_w, up_w)):
+                product = jnp.dot(expert_in[...], weight[:, source], preferred_element_type=f32)
+                if j == 0:
+                    pre_own[which, :, target] = product
+                else:
+                    pre_out[j, which, :, target] = product.astype(bf16)
+            return carry
+
+        lax.fori_loop(0, share // TILE, columns_of, 0)
+        if j:
+            copy = pltpu.make_async_remote_copy(
+                src_ref=pre_out.at[j],
+                dst_ref=pre_in.at[j],
+                send_sem=pre_send.at[j],
+                recv_sem=pre_recv.at[j],
+                device_id={"sect": partner, "dp": dp, "tp": tp},
+                device_id_type=MESH,
+            )
+            copy.start()
+            pre_copies.append(copy)
+
+    for copy in square_copies:
+        copy.wait_recv()
+    summed = square_out[:, 0:1]
+    for j in range(1, n_sect):
+        summed = summed + square_in[j, :, 0:1]
+    features = n_sect * n_tp * width
+    scale = lax.rsqrt(summed / features + norm_epsilon)
+    for copy in pre_copies:
+        copy.wait_recv()
+    gate_total, up_total = pre_own[0], pre_own[1]
+    for j in range(1, n_sect):
+        gate_total = gate_total + pre_in[j, 0].astype(f32)
+        up_total = up_total + pre_in[j, 1].astype(f32)
+    gate_total = gate_total * scale
+    act_all[sect] = (gate_total / (1.0 + jnp.exp(-gate_total)) * (up_total * scale)).astype(bf16)
+    act_copies = {}
+    for j in range(n_sect - 1, 0, -1):
+        copy = pltpu.make_async_remote_copy(
+            src_ref=act_all.at[sect],
+            dst_ref=act_all.at[sect],
+            send_sem=act_send.at[j],
+            recv_sem=act_recv.at[j],
+            device_id={"sect": flip(sect, j), "dp": dp, "tp": tp},
+            device_id_type=MESH,
+        )
+        copy.start()
+        act_copies[j] = copy
+
+    loads[3].wait()
+    pair = flip(tp, 1)
+    for j in range(n_sect):
+        if j:
+            act_copies[j].wait_recv()
+        partner = flip(sect, j)
+        last = j == n_sect - 1
+        depth = pl.ds(pl.multiple_of(partner * share, share), share)
+        for side in range(2):
+            owner = pair if side == 0 else tp
+
+            def down_columns(n, carry):
+                source = pl.ds(pl.multiple_of(owner * width + n * TILE, TILE), TILE)
+                target = pl.ds(pl.multiple_of(n * TILE, TILE), TILE)
+                product = jnp.dot(act_all[partner], down_w[depth, source], preferred_element_type=f32)
+                if j:
+                    product = product + down_own[side, :, target]
+                if last and side == 0:
+                    pair_out[:, target] = product.astype(bf16)
+                else:
+                    down_own[side, :, target] = product
+                return carry
+
+            lax.fori_loop(0, width // TILE, down_columns, 0)
+            if last and side == 0:
+                pair_copy = pltpu.make_async_remote_copy(
+                    src_ref=pair_out,
+                    dst_ref=pair_in,
+                    send_sem=pair_send,
+                    recv_sem=pair_recv,
+                    device_id={"sect": sect, "dp": dp, "tp": pair},
+                    device_id_type=MESH,
+                )
+                pair_copy.start()
+    pair_copy.wait_recv()
+    expert_out[...] = (
+        (down_own[1] + pair_in[...].astype(f32)).astype(bf16).reshape(n_dp, cap, width)
+    )
+    back_copies = []
+    for i in range(n_dp - 1, 0, -1):
+        copy = pltpu.make_async_remote_copy(
+            src_ref=expert_out.at[flip(dp, i)],
+            dst_ref=returned.at[dp],
+            send_sem=back_send.at[i],
+            recv_sem=back_recv.at[i],
+            device_id=in_line(i, 0),
+            device_id_type=MESH,
+        )
+        copy.start()
+        back_copies.append(copy)
+    returned[dp] = expert_out[dp]
+
+    for copy in stat_copies:
+        copy.wait_recv()
+    stats = stat_in[0]
+    for j in range(1, group):
+        stats = stats + stat_in[j]
+    token_scale = lax.rsqrt(stats[1, 0:1, 0:tokens] / features + norm_epsilon)
+    logits = stats[0, :, 0:tokens] * token_scale
+    chosen = [jnp.sum(logits * onehot[k], axis=0, keepdims=True) for k in range(2)]
+    weights = jnp.zeros((slots, tokens), f32)
+    for k in range(2):
+        mixing = 1.0 / (1.0 + jnp.exp(chosen[1 - k] - chosen[k]))
+        weights = weights + hit[k] * mixing
+    high = weights.astype(bf16)
+    low = (weights - high.astype(f32)).astype(bf16)
+    for copy in back_copies:
+        copy.wait_recv()
+    back = returned[...].reshape(slots, width)
+    tn = (((0,), (0,)), ((), ()))
+    combined = lax.dot_general(high, back, tn, preferred_element_type=f32) + lax.dot_general(
+        low, back, tn, preferred_element_type=f32
+    )
+    out_ref[...] = (hidden[...].astype(f32) + combined).astype(out_ref.dtype)
+
+    for copy in (
+        att_copies + row_copies + stat_copies + square_copies + pre_copies + back_copies
+    ):
+        copy.wait_send()
+    for j in range(1, n_sect):
+        act_copies[j].wait_send()
+    pair_copy.wait_send()
+
+
+def fused_layer(
+    attended, residual, out_proj, norm_gain, router, gate_proj, up_proj, down_proj, routes
+):
+    n_sect, n_dp, n_tp = (lax.axis_size(name) for name in ("sect", "dp", "tp"))
+    group = n_sect * n_tp
+    tokens, width = residual.shape
+    experts = router.shape[1]
+    cap = tokens // 2
+    slots = experts * cap
+    rows = n_dp * cap
+    share = gate_proj.shape[1] // n_sect
+    f32, bf16 = jnp.float32, jnp.bfloat16
+    vmem = pl.BlockSpec(memory_space=pltpu.VMEM)
+    hbm = pl.BlockSpec(memory_space=pl.ANY)
+    dma = pltpu.SemaphoreType.DMA
+    buffers = [
+        (out_proj.shape, bf16),
+        (gate_proj.shape, bf16),
+        (up_proj.shape, bf16),
+        (down_proj.shape, bf16),
+        ((n_tp, tokens, attended.shape[1]), bf16),
+        ((tokens, width), bf16),
+        ((2, slots, tokens), f32),
+        ((experts, cap, width), bf16),
+        ((n_tp, rows, width), bf16),
+        ((rows, n_tp * width), bf16),
+        ((rows, 128), f32),
+        ((n_sect, rows, 128), f32),
+        ((n_sect, 2, rows, share), bf16),
+        ((n_sect, 2, rows, share), bf16),
+        ((2, rows, share), f32),
+        ((n_sect, rows, share), bf16),
+        ((2, rows, width), f32),
+        ((rows, width), bf16),
+        ((rows, width), bf16),
+        ((n_dp, cap, width), bf16),
+        ((experts, cap, width), bf16),
+        ((2, 8, 128), f32),
+        ((group, 2, 8, 128), f32),
+    ]
+    semaphores = [dma((4,))]
+    for count in (group, n_dp * n_tp, group, n_sect, n_sect, n_sect):
+        semaphores += [dma((count,)), dma((count,))]
+    semaphores += [dma, dma, dma((n_dp,)), dma((n_dp,))]
+    return pl.pallas_call(
+        functools.partial(layer_kernel, (n_sect, n_dp, n_tp)),
+        out_shape=jax.ShapeDtypeStruct((tokens, width), bf16),
+        in_specs=[vmem] * 5 + [hbm] * 4,
+        out_specs=vmem,
+        scratch_shapes=[pltpu.VMEM(shape, kind) for shape, kind in buffers] + semaphores,
+        compiler_params=pltpu.CompilerParams(
+            collective_id=0, has_side_effects=True, vmem_limit_bytes=61 * 1024 * 1024
+        ),
+    )(
+        attended,
+        residual,
+        norm_gain.reshape(group, 1, width),
+        router.T,
+        routes.T,
+        out_proj,
+        gate_proj,
+        up_proj,
+        down_proj,
+    )
 
 
 def per_device(
@@ -93,6 +530,18 @@
     attended = attend(
         queries[0], key_cache[0], cached_values[0], incoming_keys[0], incoming_values[0], lengths[0]
     )
+    if lax.axis_size("tp") == 2 and residual.shape[1] % TILE == 0:
+        return fused_layer(
+            attended,
+            residual,
+            out_proj,
+            norm_gain,
+            router,
+            gate_proj[0],
+            up_proj[0],
+            down_proj[0],
+            routes,
+        )
     seq_local = attended.shape[0]
     tp_count = lax.axis_size("tp")
     head_width = attended.shape[1]

time: 199 us -> 93.1 us (0.47)
  Pallas kernels: 0 us -> 81.9 us
  waiting for transfers between devices: 72.5 us -> 0 us
  matrix products: 48.7 us -> 4.91 us
  blocking collectives: 40 us -> 0 us
  between operations: 13.4 us -> 0.04 us
  other arithmetic: 9.59 us -> 2.06 us
  starting transfers between devices: 5.12 us -> 0 us
  local copies, waits for them, and re-layouts: 8.99 us -> 3.94 us
    pallas_call x0 -> x1, Pallas kernels: none -> 81.9 us  [fused_layer(): pl.pallas_call(functools.partial(layer_kernel, (n_sect, n_dp, n_tp)), out...]
    dot_general x12 -> x0, matrix products: 45 us -> none  [the longest x8 24.5 us: add_one(): product = jnp.dot(head_block, weight, preferred_element_type=jnp.float32)]
    reduce_scatter x2 -> x0, waiting for transfers between devices: 38 us -> none  [the longest x1 33.4 us: expert_ffn(): lax.psum_scatter(pre, 'sect', scatter_dimension=4, tiled=True)]
    all_gather x1 -> x0, waiting for transfers between devices: 26.5 us -> none  [expert_ffn(): activated = lax.all_gather(share, 'sect', axis=3, tiled=True)]
    all_gather x2 -> x0, blocking collectives: 23.1 us -> none  [the longest x1 11.9 us: per_device(): shards = lax.all_gather(attended[None], ('sect', 'tp'), axis=0, tiled=True)]
    all_to_all x1 -> x0, blocking collectives: 16.9 us -> none  [per_device(): lax.all_to_all(outgoing, 'dp', split_axis=0, concat_axis=1, tiled=True)]
    all_to_all x1 -> x0, waiting for transfers between devices: 7.93 us -> none  [per_device(): lax.all_to_all(expert_ffn(lax.all_to_all(outgoing, 'dp', split_axis=0, co...]
    all_to_all x1 -> x0, starting transfers between devices: 4.85 us -> none  [per_device(): lax.all_to_all(expert_ffn(lax.all_to_all(outgoing, 'dp', split_axis=0, co...]
  transfers between devices with their start and end apart: 4 -> 0, of which waited for: 4 -> 0; matrix products, arithmetic and copies ran while one was open for 2% -> 0% of each run, Pallas kernels for 0% -> 0%
where the time goes in v2:
time: 93.1 us; the launch traced here: 92.8 us
  Pallas kernels  81.9 us (88%)
  matrix products  4.91 us (5%)
  local copies, waits for them, and re-layouts  3.94 us (4%)
  other arithmetic  2.06 us (2%)
    pallas_call x1, Pallas kernels, fused_layer(): pl.pallas_call(functools.partial(layer_kernel, (n_sect, n_dp, n_tp)), out...  81.9 us
    dot_general x1, matrix products, attend(): jnp.einsum('bkgd,bkpd->bkgp', query_head_groups, key_cache, preferred_ele...  3.7 us
    unnamed x6, local copies, waits for them, and re-layouts  3.17 us

profile of v2, /device:TPU:0, one launch (start us, length us, event | category | flops | bytes accessed | tf_op | source)
XLA Modules:
  0.0 92.8 jit_solution(619331188718555622)
XLA Ops:
  0.0 0.0 copy-start
  0.0 0.0 copy-start.1
  0.0 0.7 copy-done
  0.7 1.0 %iota_compare_fusion = pred[16,192]{1,0:T(8,128)(4,1)S(1)} fusion(s32[16]{0:T(128)} %bitcast.42), kind=kLoop, calls=%fused_computation.21 | loop fusion | flops 3072 | bytes 3136 | tf_op jit(solution)/shard_map/lt | solution.py:37
  1.7 0.7 bitcast_convert_fusion
  2.4 0.9 copy.15
  3.3 0.2 fusion.19
  3.5 3.7 %fusion.25 = (f32[16,4,6]{2,1,0:T(4,128)S(1)}, f32[16,4,6,192]{3,2,1,0:T(8,128)S(1)}) fusion(bf16[1,16,4,192,128]{4,3,2,1,0:T(8,128)(2,1)} %param.15, bf16[16,4,6,128]{3,0,2,1:T(8,128)(2,1)S(1)} %bitcast.36, pred[16,192]{1,0:T(8,128)(4,1)S(1)} %iota_compare_fusion), kind=kOutput, calls=%fused_computation.24 | convolution fusion | flops 19095168 | bytes 3543552 | tf_op jit(solution)/shard_map/bkgd,bkpd->bkgp/dot_general | solution.py:25
  7.3 0.3 fusion.16
  7.6 0.0 copy-done.1
  7.6 1.0 %fusion.13 = bf16[16,4,6,128]{3,2,1,0:T(8,128)(2,1)S(1)} fusion(bf16[1,16,4,192,128]{4,3,2,1,0:T(8,128)(2,1)S(1)} %copy-done.1, f32[16,4,6,192]{3,2,1,0:T(8,128)S(1)} %get-tuple-element.8, f32[16,4,6]{2,1,0:T(4,128)S(1)} %get-tuple-element.6, f32[16,4,6]{2,1,0:T(4,128)S(1)} %multiply_maximum_fusion, f32[16,4,128]{2,1,0:T(4,128)S(1)} %bitcast_convert_fusion, ...), kind=kOutput, calls=%fused_computation.7 | convolution fusion | flops 19243008 | bytes 3576320 | tf_op jit(solution)/shard_map/bkgp,bkpd->bkgd/dot_general | solution.py:45
  8.6 0.8 convert_element_type.30.attended_ref
  9.4 81.9 %shard_map.136 = bf16[64,768]{1,0:T(8,128)(2,1)} custom-call(bf16[16,3072]{1,0:T(8,128)(2,1)} %convert_element_type.30.attended_ref, bf16[64,768]{1,0:T(8,128)(2,1)} %residual_ref.1, f32[8,1,768]{2,1,0:T(1,128)} %bitcast.40, bf16[4,6144]{1,0:T(4,128)(2,1)} %bitcast.39, s32[2,64]{1,0:T(2,128)} %bitcast.41, bf16[6144,768]{1,0:T(8,128)(2,1)} %out_proj_hbm.1, ...), custom_call_target="tpu_custom_call" | custom-call | tf_op jit(solution)/shard_map/pallas_call | solution.py:492
  91.3 1.5 %copy.28 = bf16[64,768]{1,0:T(8,128)(2,1)} copy(bf16[64,768]{1,0:T(8,128)(2,1)} %shard_map.136) | data formatting | bytes 196608
  (2 shorter events, 0.1 us)
Async XLA Ops:
  0.0 0.7 copy-start
  0.0 7.6 %copy-start.1 = (bf16[1,16,4,192,128]{4,3,2,1,0:T(8,128)(2,1)S(1)}, bf16[1,16,4,192,128]{4,3,2,1,0:T(8,128)(2,1)}, u32[]{:S(2)}) copy-start(bf16[1,16,4,192,128]{4,3,2,1,0:T(8,128)(2,1)} %param.16) | copy-start | bytes 9437188

commit v3 on v2

--- a/solution.py
+++ b/solution.py
@@ -106,6 +106,7 @@
     pre_out,
     pre_in,
     pre_own,
+    pre_pass,
     act_all,
     down_own,
     pair_out,
@@ -153,8 +154,26 @@
         other = flip(me, j)
         return {"sect": other // n_tp, "dp": dp, "tp": other % n_tp}
 
-    def in_line(i, t):
-        return {"sect": sect, "dp": flip(dp, i), "tp": flip(tp, t)}
+    def in_sect(j):
+        return {"sect": flip(sect, j), "dp": dp, "tp": tp}
+
+    def in_line(i):
+        return {"sect": sect, "dp": flip(dp, i), "tp": tp}
+
+    pair = flip(tp, 1)
+    in_pair = {"sect": sect, "dp": dp, "tp": pair}
+
+    def send(source, target, send_sem, recv_sem, device):
+        copy = pltpu.make_async_remote_copy(
+            src_ref=source,
+            dst_ref=target,
+            send_sem=send_sem,
+            recv_sem=recv_sem,
+            device_id=device,
+            device_id_type=MESH,
+        )
+        copy.start()
+        return copy
 
     loads = []
     for index, (source, target) in enumerate(
@@ -173,25 +192,24 @@
     for j in range(1, group):
         pl.semaphore_signal(barrier, inc=1, device_id=in_group(j), device_id_type=MESH)
     for i in range(1, n_dp):
-        for t in range(n_tp):
-            pl.semaphore_signal(barrier, inc=1, device_id=in_line(i, t), device_id_type=MESH)
-    pl.semaphore_wait(barrier, group - 1 + (n_dp - 1) * n_tp)
+        pl.semaphore_signal(barrier, inc=1, device_id=in_line(i), device_id_type=MESH)
+    pl.semaphore_wait(barrier, group - 1 + n_dp - 1)
 
     seq = attended_ref.shape[0]
-    own_rows = pl.ds(pl.multiple_of(sect * seq, seq), seq)
-    att_copies = []
-    for j in range(1, group):
-        copy = pltpu.make_async_remote_copy(
-            src_ref=attended_ref,
-            dst_ref=att_all.at[tp, own_rows],
-            send_sem=att_send.at[j],
-            recv_sem=att_recv.at[j],
-            device_id=in_group(j),
-            device_id_type=MESH,
-        )
-        copy.start()
-        att_copies.append(copy)
-    att_all[tp, own_rows, :] = attended_ref[...]
+
+    def seq_rows(j):
+        return pl.ds(pl.multiple_of(flip(sect, j) * seq, seq), seq)
+
+    att_copies = {}
+    for j in range(n_sect - 1, -1, -1):
+        att_copies[j, j == 0] = send(
+            attended_ref,
+            att_all.at[tp, seq_rows(0)],
+            att_send.at[2 * j + (j == 0)],
+            att_recv.at[2 * j + (j == 0)],
+            in_sect(j) if j else in_pair,
+        )
+    att_all[tp, seq_rows(0), :] = attended_ref[...]
 
     experts = router_ref.shape[0]
     tokens = routes_ref.shape[1]
@@ -212,9 +230,15 @@
         slot = jnp.sum(rank * onehot[k], axis=0, keepdims=True).astype(jnp.int32)
         hit[k] = jnp.where(slot_ids == choice[k] * cap + slot, 1.0, 0.0).astype(f32)
 
+    for j in range(1, n_sect):
+        att_copies[j, False].wait_recv()
+        block = att_all.at[tp, seq_rows(j)]
+        att_copies[j, True] = send(
+            block, block, att_send.at[2 * j + 1], att_recv.at[2 * j + 1], in_pair
+        )
     loads[0].wait()
-    for copy in att_copies:
-        copy.wait_recv()
+    for j in range(n_sect):
+        att_copies[j, True].wait_recv()
 
     half = att_all.shape[2]
     width = out_w.shape[1]
@@ -233,23 +257,20 @@
 
     rows = jnp.dot((hit[0] + hit[1]).astype(bf16), hidden[...], preferred_element_type=f32)
     outgoing[...] = rows.astype(bf16).reshape(experts, cap, width)
-    line_rows = pl.ds(pl.multiple_of(dp * cap, cap), cap)
-    row_copies = []
+
+    def line_rows(i):
+        return pl.ds(pl.multiple_of(flip(dp, i) * cap, cap), cap)
+
+    row_copies = {}
     for i in range(n_dp - 1, -1, -1):
-        for t in range(n_tp):
-            if i == 0 and t == 0:
-                continue
-            copy = pltpu.make_async_remote_copy(
-                src_ref=outgoing.at[flip(dp, i)],
-                dst_ref=arrived.at[tp, line_rows],
-                send_sem=row_send.at[i * n_tp + t],
-                recv_sem=row_recv.at[i * n_tp + t],
-                device_id=in_line(i, t),
-                device_id_type=MESH,
-            )
-            copy.start()
-            row_copies.append(copy)
-    arrived[tp, line_rows, :] = outgoing[dp]
+        row_copies[i, i == 0] = send(
+            outgoing.at[flip(dp, i)],
+            arrived.at[tp, line_rows(0)],
+            row_send.at[2 * i + (i == 0)],
+            row_recv.at[2 * i + (i == 0)],
+            in_line(i) if i else in_pair,
+        )
+    arrived[tp, line_rows(0), :] = outgoing[dp]
 
     own = hidden[...].astype(f32)
     scaled = (own * gain_ref[me]).astype(bf16)
@@ -280,58 +301,92 @@
         stat_copies.append(copy)
     stat_in[me] = stat_out[...]
 
-    for copy in row_copies:
-        copy.wait_recv()
-
-    total_square = jnp.zeros((arrived.shape[1], 1), f32)
-    for t in range(n_tp):
+    for i in range(1, n_dp):
+        row_copies[i, False].wait_recv()
+        block = arrived.at[tp, line_rows(i)]
+        row_copies[i, True] = send(
+            block, block, row_send.at[2 * i + 1], row_recv.at[2 * i + 1], in_pair
+        )
+
+    def take(t):
         part = arrived[t].astype(f32)
-        total_square = total_square + jnp.sum(part * part, axis=1, keepdims=True)
-        expert_in[:, t * width : (t + 1) * width] = (part * gain_ref[sect * n_tp + t]).astype(bf16)
+        columns = pl.ds(pl.multiple_of(t * width, width), width)
+        expert_in[:, columns] = (part * gain_ref[sect * n_tp + t]).astype(bf16)
+        return jnp.sum(part * part, axis=1, keepdims=True)
+
+    total_square = take(tp)
+    for i in range(n_dp):
+        row_copies[i, True].wait_recv()
+    total_square = total_square + take(pair)
     square_out[...] = jnp.broadcast_to(total_square, square_out.shape)
-    square_copies = []
-    for j in range(1, n_sect):
-        copy = pltpu.make_async_remote_copy(
-            src_ref=square_out,
-            dst_ref=square_in.at[j],
-            send_sem=square_send.at[j],
-            recv_sem=square_recv.at[j],
-            device_id={"sect": flip(sect, j), "dp": dp, "tp": tp},
-            device_id_type=MESH,
-        )
-        copy.start()
-        square_copies.append(copy)
+    square_copies = [
+        send(square_out, square_in.at[j], square_send.at[j], square_recv.at[j], in_sect(j))
+        for j in range(1, n_sect)
+    ]
 
     loads[1].wait()
     loads[2].wait()
-    share = act_all.shape[2]
-    pre_copies = []
-    for j in range(n_sect - 1, -1, -1):
-        partner = flip(sect, j)
+    share = gate_w.shape[1] // n_sect
+    part_width = share // 2
+    steps = part_width // TILE
+    first, second = (1, 2), (2, 1)
+
+    def products(j, h, store):
+        start = flip(sect, j) * share + h * part_width
 
         def columns_of(n, carry):
-            source = pl.ds(pl.multiple_of(partner * share + n * TILE, TILE), TILE)
+            source = pl.ds(pl.multiple_of(start + n * TILE, TILE), TILE)
             target = pl.ds(pl.multiple_of(n * TILE, TILE), TILE)
             for which, weight in enumerate((gate_w, up_w)):
                 product = jnp.dot(expert_in[...], weight[:, source], preferred_element_type=f32)
-                if j == 0:
-                    pre_own[which, :, target] = product
-                else:
-                    pre_out[j, which, :, target] = product.astype(bf16)
+                store(which, target, product)
             return carry
 
-        lax.fori_loop(0, share // TILE, columns_of, 0)
-        if j:
-            copy = pltpu.make_async_remote_copy(
-                src_ref=pre_out.at[j],
-                dst_ref=pre_in.at[j],
-                send_sem=pre_send.at[j],
-                recv_sem=pre_recv.at[j],
-                device_id={"sect": partner, "dp": dp, "tp": tp},
-                device_id_type=MESH,
-            )
-            copy.start()
-            pre_copies.append(copy)
+        lax.fori_loop(0, steps, columns_of, 0)
+
+    def pass_on(kind, h, j):
+        index = 2 * kind + h
+        return send(
+            pre_out.at[kind, h],
+            pre_in.at[kind, h],
+            pre_send.at[index],
+            pre_recv.at[index],
+            in_sect(j),
+        )
+
+    pre_copies = {}
+    for kind in range(2):
+        for h in range(2):
+
+            def store_out(which, target, product):
+                pre_out[kind, h, which, :, target] = product.astype(bf16)
+
+            products(3 if kind == 0 else first[h], h, store_out)
+            pre_copies[kind, h] = pass_on(kind, h, first[h])
+    for h in range(2):
+
+        def store_pass(which, target, product):
+            pre_pass[h, which, :, target] = product
+
+        products(second[h], h, store_pass)
+    for h in range(2):
+        pre_copies[0, h].wait_recv()
+
+        def add_pass(n, carry):
+            target = pl.ds(pl.multiple_of(n * TILE, TILE), TILE)
+            for which in range(2):
+                total = pre_pass[h, which, :, target] + pre_in[0, h, which, :, target].astype(f32)
+                pre_out[2, h, which, :, target] = total.astype(bf16)
+            return carry
+
+        lax.fori_loop(0, steps, add_pass, 0)
+        pre_copies[2, h] = pass_on(2, h, second[h])
+    for h in range(2):
+
+        def store_own(which, target, product):
+            pre_own[h, which, :, target] = product
+
+        products(0, h, store_own)
 
     for copy in square_copies:
         copy.wait_recv()
@@ -340,43 +395,58 @@
         summed = summed + square_in[j, :, 0:1]
     features = n_sect * n_tp * width
     scale = lax.rsqrt(summed / features + norm_epsilon)
-    for copy in pre_copies:
-        copy.wait_recv()
-    gate_total, up_total = pre_own[0], pre_own[1]
-    for j in range(1, n_sect):
-        gate_total = gate_total + pre_in[j, 0].astype(f32)
-        up_total = up_total + pre_in[j, 1].astype(f32)
-    gate_total = gate_total * scale
-    act_all[sect] = (gate_total / (1.0 + jnp.exp(-gate_total)) * (up_total * scale)).astype(bf16)
     act_copies = {}
-    for j in range(n_sect - 1, 0, -1):
-        copy = pltpu.make_async_remote_copy(
-            src_ref=act_all.at[sect],
-            dst_ref=act_all.at[sect],
-            send_sem=act_send.at[j],
-            recv_sem=act_recv.at[j],
-            device_id={"sect": flip(sect, j), "dp": dp, "tp": tp},
-            device_id_type=MESH,
-        )
-        copy.start()
-        act_copies[j] = copy
+
+    def share_act(j, h, block, to):
+        index = 2 * j + h
+        act_copies[j, h] = send(
+            act_all.at[block, h],
+            act_all.at[block, h],
+            act_send.at[index],
+            act_recv.at[index],
+            in_sect(to),
+        )
+
+    for h in range(2):
+        pre_copies[1, h].wait_recv()
+        pre_copies[2, h].wait_recv()
+
+        def activate(n, carry):
+            target = pl.ds(pl.multiple_of(n * TILE, TILE), TILE)
+            sums = []
+            for which in range(2):
+                total = pre_own[h, which, :, target] + pre_in[1, h, which, :, target].astype(f32)
+                total = total + pre_in[2, h, which, :, target].astype(f32)
+                sums.append(total * scale)
+            active = sums[0] / (1.0 + jnp.exp(-sums[0])) * sums[1]
+            act_all[sect, h, :, target] = active.astype(bf16)
+            return carry
+
+        lax.fori_loop(0, steps, activate, 0)
+        share_act(first[h], h, sect, first[h])
+    for h in range(2):
+        share_act(second[h], h, sect, second[h])
 
     loads[3].wait()
-    pair = flip(tp, 1)
-    for j in range(n_sect):
+    order = ((0, 0), (0, 1), (1, 0), (2, 1), (1, 1), (2, 0), (3, 0), (3, 1))
+    for place, (j, h) in enumerate(order):
+        partner = flip(sect, j)
         if j:
-            act_copies[j].wait_recv()
-        partner = flip(sect, j)
-        last = j == n_sect - 1
-        depth = pl.ds(pl.multiple_of(partner * share, share), share)
+            act_copies[j, h].wait_recv()
+        if (j, h) in ((1, 0), (2, 1)):
+            share_act(3, h, partner, second[h])
+        last = place == len(order) - 1
+        depth = pl.ds(pl.multiple_of(partner * share + h * part_width, part_width), part_width)
         for side in range(2):
             owner = pair if side == 0 else tp
 
             def down_columns(n, carry):
                 source = pl.ds(pl.multiple_of(owner * width + n * TILE, TILE), TILE)
                 target = pl.ds(pl.multiple_of(n * TILE, TILE), TILE)
-                product = jnp.dot(act_all[partner], down_w[depth, source], preferred_element_type=f32)
-                if j:
+                product = jnp.dot(
+                    act_all[partner, h], down_w[depth, source], preferred_element_type=f32
+                )
+                if place:
                     product = product + down_own[side, :, target]
                 if last and side == 0:
                     pair_out[:, target] = product.astype(bf16)
@@ -386,31 +456,21 @@
 
             lax.fori_loop(0, width // TILE, down_columns, 0)
             if last and side == 0:
-                pair_copy = pltpu.make_async_remote_copy(
-                    src_ref=pair_out,
-                    dst_ref=pair_in,
-                    send_sem=pair_send,
-                    recv_sem=pair_recv,
-                    device_id={"sect": sect, "dp": dp, "tp": pair},
-                    device_id_type=MESH,
-                )
-                pair_copy.start()
+                pair_copy = send(pair_out, pair_in, pair_send, pair_recv, in_pair)
     pair_copy.wait_recv()
     expert_out[...] = (
         (down_own[1] + pair_in[...].astype(f32)).astype(bf16).reshape(n_dp, cap, width)
     )
-    back_copies = []
-    for i in range(n_dp - 1, 0, -1):
-        copy = pltpu.make_async_remote_copy(
-            src_ref=expert_out.at[flip(dp, i)],
-            dst_ref=returned.at[dp],
-            send_sem=back_send.at[i],
-            recv_sem=back_recv.at[i],
-            device_id=in_line(i, 0),
-            device_id_type=MESH,
-        )
-        copy.start()
-        back_copies.append(copy)
+    back_copies = [
+        send(
+            expert_out.at[flip(dp, i)],
+            returned.at[dp],
+            back_send.at[i],
+            back_recv.at[i],
+            in_line(i),
+        )
+        for i in range(n_dp - 1, 0, -1)
+    ]
     returned[dp] = expert_out[dp]
 
     for copy in stat_copies:
@@ -436,13 +496,11 @@
     )
     out_ref[...] = (hidden[...].astype(f32) + combined).astype(out_ref.dtype)
 
-    for copy in (
-        att_copies + row_copies + stat_copies + square_copies + pre_copies + back_copies
-    ):
+    for copies in (att_copies, row_copies, pre_copies, act_copies):
+        for copy in copies.values():
+            copy.wait_send()
+    for copy in stat_copies + square_copies + back_copies + [pair_copy]:
         copy.wait_send()
-    for j in range(1, n_sect):
-        act_copies[j].wait_send()
-    pair_copy.wait_send()
 
 
 def fused_layer(
@@ -473,10 +531,11 @@
         ((rows, n_tp * width), bf16),
         ((rows, 128), f32),
         ((n_sect, rows, 128), f32),
-        ((n_sect, 2, rows, share), bf16),
-        ((n_sect, 2, rows, share), bf16),
-        ((2, rows, share), f32),
-        ((n_sect, rows, share), bf16),
+        ((3, 2, 2, rows, share // 2), bf16),
+        ((3, 2, 2, rows, share // 2), bf16),
+        ((2, 2, rows, share // 2), f32),
+        ((2, 2, rows, share // 2), f32),
+        ((n_sect, 2, rows, share // 2), bf16),
         ((2, rows, width), f32),
         ((rows, width), bf16),
         ((rows, width), bf16),
@@ -486,7 +545,7 @@
         ((group, 2, 8, 128), f32),
     ]
     semaphores = [dma((4,))]
-    for count in (group, n_dp * n_tp, group, n_sect, n_sect, n_sect):
+    for count in (2 * n_sect, 2 * n_dp, group, n_sect, 6, 2 * n_sect):
         semaphores += [dma((count,)), dma((count,))]
     semaphores += [dma, dma, dma((n_dp,)), dma((n_dp,))]
     return pl.pallas_call(
@@ -530,7 +589,8 @@
     attended = attend(
         queries[0], key_cache[0], cached_values[0], incoming_keys[0], incoming_values[0], lengths[0]
     )
-    if lax.axis_size("tp") == 2 and residual.shape[1] % TILE == 0:
+    fits = lax.axis_size("sect") == 4 and lax.axis_size("tp") == 2
+    if fits and residual.shape[1] % TILE == 0:
         return fused_layer(
             attended,
             residual,

time: 93.1 us -> 77.8 us (0.84)
  Pallas kernels: 81.9 us -> 66.5 us
    pallas_call x1, Pallas kernels: 81.9 us -> 66.5 us  [fused_layer(): pl.pallas_call(functools.partial(layer_kernel, (n_sect, n_dp, n_tp)), out...]
where the time goes in v3:
time: 77.8 us; the launch traced here: 77.5 us
  Pallas kernels  66.5 us (85%)
  matrix products  4.91 us (6%)
  local copies, waits for them, and re-layouts  3.94 us (5%)
  other arithmetic  2.06 us (3%)
    pallas_call x1, Pallas kernels, fused_layer(): pl.pallas_call(functools.partial(layer_kernel, (n_sect, n_dp, n_tp)), out...  66.5 us
    dot_general x1, matrix products, attend(): jnp.einsum('bkgd,bkpd->bkgp', query_head_groups, key_cache, preferred_ele...  3.7 us
    unnamed x6, local copies, waits for them, and re-layouts  3.17 us

profile of v3, /device:TPU:0, one launch (start us, length us, event | category | flops | bytes accessed | tf_op | source)
XLA Modules:
  0.0 77.5 jit_solution(8226036458404182692)
XLA Ops:
  0.0 0.0 copy-start
  0.0 0.0 copy-start.1
  0.0 0.7 copy-done
  0.7 1.0 %iota_compare_fusion = pred[16,192]{1,0:T(8,128)(4,1)S(1)} fusion(s32[16]{0:T(128)} %bitcast.42), kind=kLoop, calls=%fused_computation.21 | loop fusion | flops 3072 | bytes 3136 | tf_op jit(solution)/shard_map/lt | solution.py:37
  1.7 0.7 bitcast_convert_fusion
  2.4 0.9 %copy.15 = bf16[1,16,24,128]{3,1,2,0:T(8,128)(2,1)S(1)} copy(bf16[1,16,24,128]{3,2,1,0:T(8,128)(2,1)} %param.14) | data formatting | bytes 196608 | tf_op args[0]
  3.3 0.2 fusion.19
  3.5 3.7 %fusion.25 = (f32[16,4,6]{2,1,0:T(4,128)S(1)}, f32[16,4,6,192]{3,2,1,0:T(8,128)S(1)}) fusion(bf16[1,16,4,192,128]{4,3,2,1,0:T(8,128)(2,1)} %param.15, bf16[16,4,6,128]{3,0,2,1:T(8,128)(2,1)S(1)} %bitcast.36, pred[16,192]{1,0:T(8,128)(4,1)S(1)} %iota_compare_fusion), kind=kOutput, calls=%fused_computation.24 | convolution fusion | flops 19095168 | bytes 3543552 | tf_op jit(solution)/shard_map/bkgd,bkpd->bkgp/dot_general | solution.py:25
  7.3 0.3 fusion.16
  7.6 0.0 copy-done.1
  7.6 1.0 %fusion.13 = bf16[16,4,6,128]{3,2,1,0:T(8,128)(2,1)S(1)} fusion(bf16[1,16,4,192,128]{4,3,2,1,0:T(8,128)(2,1)S(1)} %copy-done.1, f32[16,4,6,192]{3,2,1,0:T(8,128)S(1)} %get-tuple-element.8, f32[16,4,6]{2,1,0:T(4,128)S(1)} %get-tuple-element.6, f32[16,4,6]{2,1,0:T(4,128)S(1)} %multiply_maximum_fusion, f32[16,4,128]{2,1,0:T(4,128)S(1)} %bitcast_convert_fusion, ...), kind=kOutput, calls=%fused_computation.7 | convolution fusion | flops 19243008 | bytes 3576320 | tf_op jit(solution)/shard_map/bkgp,bkpd->bkgd/dot_general | solution.py:45
  8.6 0.8 convert_element_type.30.attended_ref
  9.4 66.5 %shard_map.136 = bf16[64,768]{1,0:T(8,128)(2,1)} custom-call(bf16[16,3072]{1,0:T(8,128)(2,1)} %convert_element_type.30.attended_ref, bf16[64,768]{1,0:T(8,128)(2,1)} %residual_ref.1, f32[8,1,768]{2,1,0:T(1,128)} %bitcast.40, bf16[4,6144]{1,0:T(4,128)(2,1)} %bitcast.39, s32[2,64]{1,0:T(2,128)} %bitcast.41, bf16[6144,768]{1,0:T(8,128)(2,1)} %out_proj_hbm.1, ...), custom_call_target="tpu_custom_call" | custom-call | tf_op jit(solution)/shard_map/pallas_call | solution.py:551
  75.9 1.5 %copy.28 = bf16[64,768]{1,0:T(8,128)(2,1)} copy(bf16[64,768]{1,0:T(8,128)(2,1)} %shard_map.136) | data formatting | bytes 196608
  (2 shorter events, 0.1 us)
Async XLA Ops:
  0.0 0.7 copy-start
  0.0 7.6 %copy-start.1 = (bf16[1,16,4,192,128]{4,3,2,1,0:T(8,128)(2,1)S(1)}, bf16[1,16,4,192,128]{4,3,2,1,0:T(8,128)(2,1)}, u32[]{:S(2)}) copy-start(bf16[1,16,4,192,128]{4,3,2,1,0:T(8,128)(2,1)} %param.16) | copy-start | bytes 9437188

commit v4 on v3

--- a/solution.py
+++ b/solution.py
@@ -81,16 +81,25 @@
 
 def layer_kernel(
     sizes,
-    attended_ref,
+    queries_ref,
+    fresh_keys_ref,
+    fresh_values_ref,
+    lengths_ref,
     residual_ref,
     gain_ref,
     router_ref,
     routes_ref,
+    keys_hbm,
+    values_hbm,
     out_proj_hbm,
     gate_hbm,
     up_hbm,
     down_hbm,
     out_ref,
+    keys,
+    values,
+    by_token,
+    attended,
     out_w,
     gate_w,
     up_w,
@@ -106,7 +115,6 @@
     pre_out,
     pre_in,
     pre_own,
-    pre_pass,
     act_all,
     down_own,
     pair_out,
@@ -115,6 +123,7 @@
     returned,
     stat_out,
     stat_in,
+    cache_sem,
     weight_sem,
     att_send,
     att_recv,
@@ -175,6 +184,17 @@
         copy.start()
         return copy
 
+    seq, query_heads, head_size = queries_ref.shape
+    pieces = 4
+    cache_loads = []
+    for piece in range(pieces):
+        span = pl.ds(piece * (seq // pieces), seq // pieces)
+        for which, (source, target) in enumerate(((keys_hbm, keys), (values_hbm, values))):
+            copy = pltpu.make_async_copy(
+                source.at[span], target.at[span], cache_sem.at[which, piece]
+            )
+            copy.start()
+            cache_loads.append(copy)
     loads = []
     for index, (source, target) in enumerate(
         ((out_proj_hbm, out_w), (gate_hbm, gate_w), (up_hbm, up_w), (down_hbm, down_w))
@@ -193,9 +213,66 @@
         pl.semaphore_signal(barrier, inc=1, device_id=in_group(j), device_id_type=MESH)
     for i in range(1, n_dp):
         pl.semaphore_signal(barrier, inc=1, device_id=in_line(i), device_id_type=MESH)
+
+    kv_heads, context = keys.shape[1], keys.shape[2]
+    per_group = query_heads // kv_heads
+    every = kv_heads * context
+    nt = (((1,), (1,)), ((), ()))
+    head_of_row = lax.broadcasted_iota(jnp.int32, (query_heads, every), 0) // per_group
+    slot_of_column = lax.broadcasted_iota(jnp.int32, (query_heads, every), 1)
+    head_of_column = slot_of_column // context
+    position = jnp.where(
+        head_of_row == head_of_column, slot_of_column - head_of_column * context, context
+    )
+    fresh_same = (
+        lax.broadcasted_iota(jnp.int32, (query_heads, kv_heads), 0) // per_group
+    ) == lax.broadcasted_iota(jnp.int32, (query_heads, kv_heads), 1)
+    logit_scale = 1.0 / math.sqrt(head_size)
+
+    def attend_token(b):
+        query = queries_ref[b]
+        scores = lax.dot_general(
+            query, keys[b].reshape(every, head_size), nt, preferred_element_type=f32
+        )
+        fresh = lax.dot_general(query, fresh_keys_ref[b], nt, preferred_element_type=f32)
+        scores = jnp.where(position < lengths_ref[0, b], scores * logit_scale, -jnp.inf)
+        fresh = jnp.where(fresh_same, fresh * logit_scale, -jnp.inf)
+        highest = jnp.maximum(
+            jnp.max(scores, axis=1, keepdims=True), jnp.max(fresh, axis=1, keepdims=True)
+        )
+        scores = jnp.exp(scores - highest)
+        fresh = jnp.exp(fresh - highest)
+        total = jnp.sum(scores, axis=1, keepdims=True) + jnp.sum(fresh, axis=1, keepdims=True)
+        inverse = 1.0 / total
+        probs = (scores * inverse).astype(bf16)
+        fresh_probs = (fresh * inverse).astype(bf16)
+        mixed = jnp.dot(probs, values[b].reshape(every, head_size), preferred_element_type=f32)
+        fresh_part = jnp.dot(fresh_probs, fresh_values_ref[b], preferred_element_type=f32)
+        return mixed + fresh_part
+
+    step = seq // pieces
+    for piece in range(pieces):
+        cache_loads[2 * piece].wait()
+        cache_loads[2 * piece + 1].wait()
+
+        def attend_step(b, carry):
+            by_token[b] = attend_token(b)
+            return carry
+
+        lax.fori_loop(piece * step, (piece + 1) * step, attend_step, 0, unroll=True)
+    count = seq * query_heads
+    row = lax.broadcasted_iota(jnp.int32, (count, count), 0)
+    column = lax.broadcasted_iota(jnp.int32, (count, count), 1)
+    source = (row % seq) * query_heads + row // seq
+    order = jnp.where(column == source, 1.0, 0.0).astype(bf16)
+    rows_by_token = by_token[...].reshape(count, head_size).astype(bf16)
+    attended[...] = (
+        jnp.dot(order, rows_by_token, preferred_element_type=f32)
+        .astype(bf16)
+        .reshape(query_heads, seq, head_size)
+    )
     pl.semaphore_wait(barrier, group - 1 + n_dp - 1)
 
-    seq = attended_ref.shape[0]
 
     def seq_rows(j):
         return pl.ds(pl.multiple_of(flip(sect, j) * seq, seq), seq)
@@ -203,13 +280,13 @@
     att_copies = {}
     for j in range(n_sect - 1, -1, -1):
         att_copies[j, j == 0] = send(
-            attended_ref,
-            att_all.at[tp, seq_rows(0)],
+            attended,
+            att_all.at[tp, :, seq_rows(0)],
             att_send.at[2 * j + (j == 0)],
             att_recv.at[2 * j + (j == 0)],
             in_sect(j) if j else in_pair,
         )
-    att_all[tp, seq_rows(0), :] = attended_ref[...]
+    att_all[tp, :, seq_rows(0), :] = attended[...]
 
     experts = router_ref.shape[0]
     tokens = routes_ref.shape[1]
@@ -232,7 +309,7 @@
 
     for j in range(1, n_sect):
         att_copies[j, False].wait_recv()
-        block = att_all.at[tp, seq_rows(j)]
+        block = att_all.at[tp, :, seq_rows(j)]
         att_copies[j, True] = send(
             block, block, att_send.at[2 * j + 1], att_recv.at[2 * j + 1], in_pair
         )
@@ -240,15 +317,16 @@
     for j in range(n_sect):
         att_copies[j, True].wait_recv()
 
-    half = att_all.shape[2]
+    half = query_heads * head_size
     width = out_w.shape[1]
 
     def project(n, carry):
         columns = pl.ds(pl.multiple_of(n * TILE, TILE), TILE)
         total = residual_ref[:, columns].astype(f32)
         for t in range(n_tp):
+            heads = jnp.concatenate([att_all[t, head] for head in range(query_heads)], axis=1)
             total = total + jnp.dot(
-                att_all[t], out_w[t * half : (t + 1) * half, columns], preferred_element_type=f32
+                heads, out_w[t * half : (t + 1) * half, columns], preferred_element_type=f32
             )
         hidden[:, columns] = total.astype(bf16)
         return carry
@@ -366,7 +444,7 @@
     for h in range(2):
 
         def store_pass(which, target, product):
-            pre_pass[h, which, :, target] = product
+            pre_own[h, which, :, target] = product
 
         products(second[h], h, store_pass)
     for h in range(2):
@@ -375,7 +453,7 @@
         def add_pass(n, carry):
             target = pl.ds(pl.multiple_of(n * TILE, TILE), TILE)
             for which in range(2):
-                total = pre_pass[h, which, :, target] + pre_in[0, h, which, :, target].astype(f32)
+                total = pre_own[h, which, :, target] + pre_in[0, h, which, :, target].astype(f32)
                 pre_out[2, h, which, :, target] = total.astype(bf16)
             return carry
 
@@ -504,7 +582,20 @@
 
 
 def fused_layer(
-    attended, residual, out_proj, norm_gain, router, gate_proj, up_proj, down_proj, routes
+    queries,
+    key_cache,
+    cached_values,
+    incoming_keys,
+    incoming_values,
+    lengths,
+    residual,
+    out_proj,
+    norm_gain,
+    router,
+    gate_proj,
+    up_proj,
+    down_proj,
+    routes,
 ):
     n_sect, n_dp, n_tp = (lax.axis_size(name) for name in ("sect", "dp", "tp"))
     group = n_sect * n_tp
@@ -518,12 +609,17 @@
     vmem = pl.BlockSpec(memory_space=pltpu.VMEM)
     hbm = pl.BlockSpec(memory_space=pl.ANY)
     dma = pltpu.SemaphoreType.DMA
+    seq, heads, head_size = queries.shape
     buffers = [
+        (key_cache.shape, bf16),
+        (cached_values.shape, bf16),
+        (queries.shape, f32),
+        ((heads, seq, head_size), bf16),
         (out_proj.shape, bf16),
         (gate_proj.shape, bf16),
         (up_proj.shape, bf16),
         (down_proj.shape, bf16),
-        ((n_tp, tokens, attended.shape[1]), bf16),
+        ((n_tp, heads, tokens, head_size), bf16),
         ((tokens, width), bf16),
         ((2, slots, tokens), f32),
         ((experts, cap, width), bf16),
@@ -534,7 +630,6 @@
         ((3, 2, 2, rows, share // 2), bf16),
         ((3, 2, 2, rows, share // 2), bf16),
         ((2, 2, rows, share // 2), f32),
-        ((2, 2, rows, share // 2), f32),
         ((n_sect, 2, rows, share // 2), bf16),
         ((2, rows, width), f32),
         ((rows, width), bf16),
@@ -544,25 +639,33 @@
         ((2, 8, 128), f32),
         ((group, 2, 8, 128), f32),
     ]
-    semaphores = [dma((4,))]
+    semaphores = [dma((2, 4)), dma((4,))]
     for count in (2 * n_sect, 2 * n_dp, group, n_sect, 6, 2 * n_sect):
         semaphores += [dma((count,)), dma((count,))]
     semaphores += [dma, dma, dma((n_dp,)), dma((n_dp,))]
     return pl.pallas_call(
         functools.partial(layer_kernel, (n_sect, n_dp, n_tp)),
         out_shape=jax.ShapeDtypeStruct((tokens, width), bf16),
-        in_specs=[vmem] * 5 + [hbm] * 4,
+        in_specs=[vmem] * 3
+        + [pl.BlockSpec(memory_space=pltpu.SMEM)]
+        + [vmem] * 4
+        + [hbm] * 6,
         out_specs=vmem,
         scratch_shapes=[pltpu.VMEM(shape, kind) for shape, kind in buffers] + semaphores,
         compiler_params=pltpu.CompilerParams(
-            collective_id=0, has_side_effects=True, vmem_limit_bytes=61 * 1024 * 1024
+            collective_id=0, has_side_effects=True, vmem_limit_bytes=62 * 1024 * 1024
         ),
     )(
-        attended,
+        queries,
+        incoming_keys,
+        incoming_values,
+        lengths,
         residual,
         norm_gain.reshape(group, 1, width),
         router.T,
         routes.T,
+        key_cache,
+        cached_values,
         out_proj,
         gate_proj,
         up_proj,
@@ -586,13 +689,15 @@
     down_proj,
     routes,
 ):
-    attended = attend(
-        queries[0], key_cache[0], cached_values[0], incoming_keys[0], incoming_values[0], lengths[0]
-    )
     fits = lax.axis_size("sect") == 4 and lax.axis_size("tp") == 2
     if fits and residual.shape[1] % TILE == 0:
         return fused_layer(
-            attended,
+            queries[0],
+            key_cache[0],
+            cached_values[0],
+            incoming_keys[0],
+            incoming_values[0],
+            lengths,
             residual,
             out_proj,
             norm_gain,
@@ -602,6 +707,9 @@
             down_proj[0],
             routes,
         )
+    attended = attend(
+        queries[0], key_cache[0], cached_values[0], incoming_keys[0], incoming_values[0], lengths[0]
+    )
     seq_local = attended.shape[0]
     tp_count = lax.axis_size("tp")
     head_width = attended.shape[1]

time: 77.8 us -> 83.6 us (1.075)
  Pallas kernels: 66.5 us -> 81.9 us
  matrix products: 4.91 us -> 0 us
  local copies, waits for them, and re-layouts: 3.94 us -> 1.54 us
  other arithmetic: 2.06 us -> 0 us
    pallas_call x1, Pallas kernels: 66.5 us -> 81.9 us  [fused_layer(): pl.pallas_call(functools.partial(layer_kernel, (n_sect, n_dp, n_tp)), out...]
    dot_general x3 -> x0, matrix products: 4.91 us -> none  [the longest x1 3.7 us: attend(): jnp.einsum('bkgd,bkpd->bkgp', query_head_groups, key_cache, preferred_ele...]
    unnamed x6 -> x1, local copies, waits for them, and re-layouts: 3.17 us -> 1.54 us
    lt x1 -> x0, other arithmetic: 0.97 us -> none  [attend(): valid_slots = positions[None, :] < lengths[:, None]]
where the time goes in v4:
time: 83.6 us; the launch traced here: 83.4 us
  Pallas kernels  81.9 us (98%)
  local copies, waits for them, and re-layouts  1.54 us (2%)
    pallas_call x1, Pallas kernels, fused_layer(): pl.pallas_call(functools.partial(layer_kernel, (n_sect, n_dp, n_tp)), out...  81.9 us

profile of v4, /device:TPU:0, one launch (start us, length us, event | category | flops | bytes accessed | tf_op | source)
XLA Modules:
  0.0 83.4 jit_solution(14287650264586630219)
XLA Ops:
  0.0 81.9 %shard_map.136 = bf16[64,768]{1,0:T(8,128)(2,1)} custom-call(bf16[16,24,128]{2,1,0:T(8,128)(2,1)} %bitcast.16, bf16[16,4,128]{2,1,0:T(4,128)(2,1)} %bitcast.19, bf16[16,4,128]{2,1,0:T(4,128)(2,1)} %bitcast.20, s32[1,16]{1,0:T(1,128)} %lengths_ref.1, bf16[64,768]{1,0:T(8,128)(2,1)} %residual_ref.1, f32[8,1,768]{2,1,0:T(1,128)} %bitcast.18, ...), custom_call_target="tpu_custom_call" | custom-call | tf_op jit(solution)/shard_map/pallas_call | solution.py:646
  81.9 1.5 %copy.16 = bf16[64,768]{1,0:T(8,128)(2,1)} copy(bf16[64,768]{1,0:T(8,128)(2,1)} %shard_map.136) | data formatting | bytes 196608

commit v5 on v4

--- a/solution.py
+++ b/solution.py
@@ -195,18 +195,21 @@
             )
             copy.start()
             cache_loads.append(copy)
-    loads = []
-    for index, (source, target) in enumerate(
-        ((out_proj_hbm, out_w), (gate_hbm, gate_w), (up_hbm, up_w), (down_hbm, down_w))
-    ):
-        rows = source.shape[0] // 4
+    weights = ((out_proj_hbm, out_w), (gate_hbm, gate_w), (up_hbm, up_w), (down_hbm, down_w))
+
+    def load(index):
+        source, target = weights[index]
+        depth = source.shape[0] // 4
         for part in range(4):
             pltpu.make_async_copy(
-                source.at[pl.ds(part * rows, rows)],
-                target.at[pl.ds(part * rows, rows)],
+                source.at[pl.ds(part * depth, depth)],
+                target.at[pl.ds(part * depth, depth)],
                 weight_sem.at[index],
             ).start()
-        loads.append(pltpu.make_async_copy(source, target, weight_sem.at[index]))
+
+    def loaded(index):
+        source, target = weights[index]
+        pltpu.make_async_copy(source, target, weight_sem.at[index]).wait()
 
     barrier = pltpu.get_barrier_semaphore()
     for j in range(1, group):
@@ -229,14 +232,28 @@
     ) == lax.broadcasted_iota(jnp.int32, (query_heads, kv_heads), 1)
     logit_scale = 1.0 / math.sqrt(head_size)
 
-    def attend_token(b):
-        query = queries_ref[b]
-        scores = lax.dot_general(
-            query, keys[b].reshape(every, head_size), nt, preferred_element_type=f32
-        )
-        fresh = lax.dot_general(query, fresh_keys_ref[b], nt, preferred_element_type=f32)
-        scores = jnp.where(position < lengths_ref[0, b], scores * logit_scale, -jnp.inf)
-        fresh = jnp.where(fresh_same, fresh * logit_scale, -jnp.inf)
+    step = seq // pieces
+
+    def rows_of(array, place):
+        return array[place * query_heads : (place + 1) * query_heads]
+
+    for piece in range(pieces):
+        cache_loads[2 * piece].wait()
+        cache_loads[2 * piece + 1].wait()
+        if piece == pieces - 2:
+            load(0)
+        batch = range(piece * step, (piece + 1) * step)
+        scores, fresh = [], []
+        for b in batch:
+            query = queries_ref[b]
+            score = lax.dot_general(
+                query, keys[b].reshape(every, head_size), nt, preferred_element_type=f32
+            )
+            scores.append(jnp.where(position < lengths_ref[0, b], score * logit_scale, -jnp.inf))
+            score = lax.dot_general(query, fresh_keys_ref[b], nt, preferred_element_type=f32)
+            fresh.append(jnp.where(fresh_same, score * logit_scale, -jnp.inf))
+        scores = jnp.concatenate(scores, axis=0)
+        fresh = jnp.concatenate(fresh, axis=0)
         highest = jnp.maximum(
             jnp.max(scores, axis=1, keepdims=True), jnp.max(fresh, axis=1, keepdims=True)
         )
@@ -244,22 +261,17 @@
         fresh = jnp.exp(fresh - highest)
         total = jnp.sum(scores, axis=1, keepdims=True) + jnp.sum(fresh, axis=1, keepdims=True)
         inverse = 1.0 / total
-        probs = (scores * inverse).astype(bf16)
-        fresh_probs = (fresh * inverse).astype(bf16)
-        mixed = jnp.dot(probs, values[b].reshape(every, head_size), preferred_element_type=f32)
-        fresh_part = jnp.dot(fresh_probs, fresh_values_ref[b], preferred_element_type=f32)
-        return mixed + fresh_part
-
-    step = seq // pieces
-    for piece in range(pieces):
-        cache_loads[2 * piece].wait()
-        cache_loads[2 * piece + 1].wait()
-
-        def attend_step(b, carry):
-            by_token[b] = attend_token(b)
-            return carry
-
-        lax.fori_loop(piece * step, (piece + 1) * step, attend_step, 0, unroll=True)
+        scores = scores * inverse
+        fresh = fresh * inverse
+        for place, b in enumerate(batch):
+            by_token[b] = jnp.dot(
+                rows_of(scores, place).astype(bf16),
+                values[b].reshape(every, head_size),
+                preferred_element_type=f32,
+            ) + jnp.dot(
+                rows_of(fresh, place).astype(bf16), fresh_values_ref[b], preferred_element_type=f32
+            )
+
     count = seq * query_heads
     row = lax.broadcasted_iota(jnp.int32, (count, count), 0)
     column = lax.broadcasted_iota(jnp.int32, (count, count), 1)
@@ -287,6 +299,8 @@
             in_sect(j) if j else in_pair,
         )
     att_all[tp, :, seq_rows(0), :] = attended[...]
+
+    load(1)
 
     experts = router_ref.shape[0]
     tokens = routes_ref.shape[1]
@@ -313,7 +327,8 @@
         att_copies[j, True] = send(
             block, block, att_send.at[2 * j + 1], att_recv.at[2 * j + 1], in_pair
         )
-    loads[0].wait()
+    loaded(0)
+    load(2)
     for j in range(n_sect):
         att_copies[j, True].wait_recv()
 
@@ -402,8 +417,9 @@
         for j in range(1, n_sect)
     ]
 
-    loads[1].wait()
-    loads[2].wait()
+    loaded(1)
+    loaded(2)
+    load(3)
     share = gate_w.shape[1] // n_sect
     part_width = share // 2
     steps = part_width // TILE
@@ -505,7 +521,7 @@
     for h in range(2):
         share_act(second[h], h, sect, second[h])
 
-    loads[3].wait()
+    loaded(3)
     order = ((0, 0), (0, 1), (1, 0), (2, 1), (1, 1), (2, 0), (3, 0), (3, 1))
     for place, (j, h) in enumerate(order):
         partner = flip(sect, j)

time: 83.6 us -> 70.6 us (0.84)
  Pallas kernels: 81.9 us -> 68.9 us
    pallas_call x1, Pallas kernels: 81.9 us -> 68.9 us  [fused_layer(): pl.pallas_call(functools.partial(layer_kernel, (n_sect, n_dp, n_tp)), out...]
where the time goes in v5:
time: 70.6 us; the launch traced here: 70.4 us
  Pallas kernels  68.9 us (98%)
  local copies, waits for them, and re-layouts  1.54 us (2%)
    pallas_call x1, Pallas kernels, fused_layer(): pl.pallas_call(functools.partial(layer_kernel, (n_sect, n_dp, n_tp)), out...  68.9 us
    unnamed x1, local copies, waits for them, and re-layouts  1.54 us

profile of v5, /device:TPU:0, one launch (start us, length us, event | category | flops | bytes accessed | tf_op | source)
XLA Modules:
  0.0 70.4 jit_solution(9630679169516313124)
XLA Ops:
  0.0 68.9 %shard_map.136 = bf16[64,768]{1,0:T(8,128)(2,1)} custom-call(bf16[16,24,128]{2,1,0:T(8,128)(2,1)} %bitcast.16, bf16[16,4,128]{2,1,0:T(4,128)(2,1)} %bitcast.19, bf16[16,4,128]{2,1,0:T(4,128)(2,1)} %bitcast.20, s32[1,16]{1,0:T(1,128)} %lengths_ref.1, bf16[64,768]{1,0:T(8,128)(2,1)} %residual_ref.1, f32[8,1,768]{2,1,0:T(1,128)} %bitcast.18, ...), custom_call_target="tpu_custom_call" | custom-call | tf_op jit(solution)/shard_map/pallas_call | solution.py:662
  68.9 1.5 %copy.16 = bf16[64,768]{1,0:T(8,128)(2,1)} copy(bf16[64,768]{1,0:T(8,128)(2,1)} %shard_map.136) | data formatting | bytes 196608

commit v6 on v5

--- a/solution.py
+++ b/solution.py
@@ -193,7 +193,8 @@
             copy = pltpu.make_async_copy(
                 source.at[span], target.at[span], cache_sem.at[which, piece]
             )
-            copy.start()
+            if piece < 2:
+                copy.start()
             cache_loads.append(copy)
     weights = ((out_proj_hbm, out_w), (gate_hbm, gate_w), (up_hbm, up_w), (down_hbm, down_w))
 
@@ -240,6 +241,9 @@
     for piece in range(pieces):
         cache_loads[2 * piece].wait()
         cache_loads[2 * piece + 1].wait()
+        if piece < pieces - 2:
+            cache_loads[2 * piece + 4].start()
+            cache_loads[2 * piece + 5].start()
         if piece == pieces - 2:
             load(0)
         batch = range(piece * step, (piece + 1) * step)
@@ -523,15 +527,17 @@
 
     loaded(3)
     order = ((0, 0), (0, 1), (1, 0), (2, 1), (1, 1), (2, 0), (3, 0), (3, 1))
-    for place, (j, h) in enumerate(order):
+    rounds = [(unit, (0, 1)) for unit in order[:-2]]
+    rounds += [(unit, (side,)) for side in range(2) for unit in order[-2:]]
+    for place, ((j, h), sides) in enumerate(rounds):
         partner = flip(sect, j)
-        if j:
+        if j and sides != (1,):
             act_copies[j, h].wait_recv()
         if (j, h) in ((1, 0), (2, 1)):
             share_act(3, h, partner, second[h])
-        last = place == len(order) - 1
+        last = (j, h) == order[-1]
         depth = pl.ds(pl.multiple_of(partner * share + h * part_width, part_width), part_width)
-        for side in range(2):
+        for side in sides:
             owner = pair if side == 0 else tp
 
             def down_columns(n, carry):

time: 70.6 us -> 70.4 us (level)
  no operation moved by 1% of the time
where the time goes in v6:
time: 70.4 us; the launch traced here: 70.2 us
  Pallas kernels  68.7 us (98%)
  local copies, waits for them, and re-layouts  1.54 us (2%)
    pallas_call x1, Pallas kernels, fused_layer(): pl.pallas_call(functools.partial(layer_kernel, (n_sect, n_dp, n_tp)), out...  68.7 us
    unnamed x1, local copies, waits for them, and re-layouts  1.54 us

profile of v6, /device:TPU:0, one launch (start us, length us, event | category | flops | bytes accessed | tf_op | source)
XLA Modules:
  0.0 70.2 jit_solution(9390488772242221638)
XLA Ops:
  0.0 68.7 %shard_map.136 = bf16[64,768]{1,0:T(8,128)(2,1)} custom-call(bf16[16,24,128]{2,1,0:T(8,128)(2,1)} %bitcast.16, bf16[16,4,128]{2,1,0:T(4,128)(2,1)} %bitcast.19, bf16[16,4,128]{2,1,0:T(4,128)(2,1)} %bitcast.20, s32[1,16]{1,0:T(1,128)} %lengths_ref.1, bf16[64,768]{1,0:T(8,128)(2,1)} %residual_ref.1, f32[8,1,768]{2,1,0:T(1,128)} %bitcast.18, ...), custom_call_target="tpu_custom_call" | custom-call | tf_op jit(solution)/shard_map/pallas_call | solution.py:668
  68.7 1.5 %copy.16 = bf16[64,768]{1,0:T(8,128)(2,1)} copy(bf16[64,768]{1,0:T(8,128)(2,1)} %shard_map.136) | data formatting | bytes 196608
